TPU v7x, 32 devices: a whole 2x2x4 slice. The times are simulated.
32 devices in a mesh: tm: 8 (over z, x), chan: 4 (over y, core).
Axes of the slice: x: 2, y: 2, z: 4, core: 2. Of those that a mesh axis runs over, the one named last changes fastest.
Arguments:
- traces: float32 [4096, 16384], P('tm', 'chan'), may hold values from -6 to 6
- band_edges: int32 [2, 4096], replicated, may hold values from 0 to 8191, as said below
- taps: float32 [255], replicated, may hold values from -0.375 to 0.375
- gain_table: float32 [64], replicated, may hold values from 0.3 to 3
- gain_index: int32 [16384], P('chan'), may hold values from 0 to 63
Outputs:
- filtered: float32 [4096, 16384], P('tm', 'chan')
Inputs may be any that keep to these rules, and one draw needn't show every extreme that they name: band_edges[0, f] <= band_edges[1, f] for every f.
All inputs are finite; a program needn't handle non-finite values.
Results may differ from a plain program's by a relative error of at most 0.0001.
Values sent between devices are 32-bit elements; how exact they have to be, the bound alone decides.
A program may use at most 128 MiB of HBM per device.

v0:
```python
import math

import jax
import jax.numpy as jnp
from jax import lax
from jax.sharding import PartitionSpec as P

highest = lax.Precision.HIGHEST


def extended(cells, sides, width):
    for axis, dim in sides:
        count = lax.axis_size(axis)
        ends = count - 1
        head = lax.slice_in_dim(cells, 0, width, axis=dim)
        tail = lax.slice_in_dim(cells, cells.shape[dim] - width, cells.shape[dim], axis=dim)
        cells = jnp.concatenate(
            [
                lax.ppermute(tail, axis, [(i, (i + 1) % count) for i in range(ends)]),
                cells,
                lax.ppermute(head, axis, [((i + 1) % count, i) for i in range(ends)]),
            ],
            axis=dim,
        )
    return cells


def split_length(total):
    bits = total.bit_length() - 1
    outer = 2 ** ((bits + 1) // 2)
    return (total // outer, outer)


def angles(rows, cols, period):
    product = (
        jnp.arange(rows, dtype=jnp.int32)[:, None]
        * jnp.arange(cols, dtype=jnp.int32)[None, :]
        % period
    )
    theta = product.astype(jnp.float32) * (2.0 * math.pi / period)
    return (jnp.cos(theta), jnp.sin(theta))


def channel_forward(values, count):
    rows, length = values.shape
    inner, outer = split_length(length)
    block = values.reshape(rows, outer, inner)
    cos_b, sin_b = angles(outer, outer, outer)
    first_table = jnp.stack([cos_b, -sin_b], axis=1)
    first = jnp.einsum("rba,bsg->rsga", block, first_table, precision=highest)
    real_part = first[:, 0]
    imag_part = first[:, 1]
    cos_t, sin_t = angles(outer, inner, length)
    turned = jnp.stack(
        [real_part * cos_t + imag_part * sin_t, imag_part * cos_t - real_part * sin_t], axis=1
    )
    higher = count // outer
    cos_a, sin_a = angles(inner, higher, inner)
    last_table = jnp.stack(
        [jnp.stack([cos_a, -sin_a], axis=1), jnp.stack([sin_a, cos_a], axis=1)], axis=0
    )
    result = jnp.einsum("rsga,saph->rphg", turned, last_table, precision=highest)
    return (result[:, 0].reshape(rows, count), result[:, 1].reshape(rows, count))


def channel_inverse(stacked, length):
    rows, count = (stacked.shape[0], stacked.shape[2])
    inner, outer = split_length(length)
    higher = count // outer
    blocks = stacked.reshape(rows, 2, higher, outer)
    cos_a, sin_a = angles(higher, inner, inner)
    first_table = jnp.stack(
        [jnp.stack([cos_a, sin_a], axis=1), jnp.stack([-sin_a, cos_a], axis=1)], axis=0
    )
    wide = jnp.einsum("rshg,shpa->rpga", blocks, first_table, precision=highest)
    wide_real = wide[:, 0]
    wide_imag = wide[:, 1]
    cos_t, sin_t = angles(outer, inner, length)
    turned = jnp.stack(
        [wide_real * cos_t - wide_imag * sin_t, wide_imag * cos_t + wide_real * sin_t], axis=1
    )
    cos_b, sin_b = angles(outer, outer, outer)
    last_table = jnp.stack([cos_b, -sin_b], axis=0)
    result = jnp.einsum("rsga,sgb->rba", turned, last_table, precision=highest)
    return result.reshape(rows, length)


def swapped(values, half):
    return jnp.concatenate([values[..., half:], values[..., :half]], axis=-1)


def time_transform(stacked, direction):
    length, width = stacked.shape
    half = width // 2
    inner, outer = split_length(length)
    sign_row = jnp.concatenate(
        [jnp.full((half,), -direction, jnp.float32), jnp.full((half,), direction, jnp.float32)]
    )
    block = stacked.reshape(outer, inner, width)
    cos_b, sin_b = angles(outer, outer, outer)
    first = (
        jnp.einsum("gb,bac->gac", cos_b, block, precision=highest)
        + swapped(jnp.einsum("gb,bac->gac", sin_b, block, precision=highest), half) * sign_row
    )
    cos_t, sin_t = angles(outer, inner, length)
    turned = first * cos_t[:, :, None] + swapped(first, half) * sign_row * sin_t[:, :, None]
    cos_a, sin_a = angles(inner, inner, inner)
    second = (
        jnp.einsum("ha,gac->hgc", cos_a, turned, precision=highest)
        + swapped(jnp.einsum("ha,gac->hgc", sin_a, turned, precision=highest), half) * sign_row
    )
    return second.reshape(length, width)


def mask_factor(band_edges, samples, channels, piece):
    owner = lax.axis_index("tm") * lax.axis_size("chan") + lax.axis_index("chan")
    wave = owner * piece + jnp.arange(piece, dtype=jnp.int32)[None, :]
    kept = (wave >= band_edges[0][:, None]) & (wave <= band_edges[1][:, None])
    weight = jnp.where(wave == 0, 1.0, 2.0).astype(jnp.float32)
    factor = jnp.where(kept, weight, 0.0) / float(samples * channels)
    return jnp.concatenate([factor, factor], axis=1)


def toeplitz_tiles(taps):
    count = taps.shape[0]
    centre = (count - 1) // 2
    before = 256 - centre
    after = 512 - before - count
    widened = jnp.concatenate(
        [jnp.zeros((before,), jnp.float32), taps, jnp.zeros((after,), jnp.float32)]
    )
    tiles = []
    for shift in range(3):
        start = 128 * shift + 128
        reversed_part = widened[start - 127 : start + 128][::-1]
        rolled = jnp.concatenate(
            [reversed_part[127:], jnp.zeros((1,), jnp.float32), reversed_part[:127]]
        )
        tiled = jnp.tile(rolled, 128)[: 128 * 255].reshape(128, 255)
        tiles.append(tiled[:, :128])
    return jnp.stack(tiles)


def apply_tiles(padded, taps, length):
    width = padded.shape[1]
    tiles = length // 128
    blocks = padded.reshape(tiles + 2, 128, width)
    kernels = toeplitz_tiles(taps)
    total = jnp.zeros((tiles, 128, width), jnp.float32)
    for shift in range(3):
        total = total + jnp.einsum(
            "ab,jac->jbc", kernels[shift], blocks[shift : shift + tiles], precision=highest
        )
    return total.reshape(length, width)


def bandpass(local, taps):
    length = local.shape[0]
    padded = extended(local, (("tm", 0),), 128)
    return apply_tiles(padded, taps, length)


def per_device(traces, band_edges, taps, gain_table, gain_index):
    gathered = lax.all_to_all(traces, "chan", split_axis=0, concat_axis=1, tiled=True)
    rows, channels = gathered.shape
    count = channels // 2
    real_part, imag_part = channel_forward(gathered, count)
    devices = lax.axis_size("tm") * lax.axis_size("chan")
    piece = count // devices
    packed = jnp.stack(
        [real_part.reshape(rows, devices, piece), imag_part.reshape(rows, devices, piece)], axis=2
    )
    packed = packed.reshape(1, rows, devices * 2 * piece)
    spectra = lax.all_to_all(
        lax.all_to_all(packed, "tm", split_axis=2, concat_axis=0, tiled=True),
        "chan",
        split_axis=2,
        concat_axis=1,
        tiled=True,
    )
    samples = spectra.shape[0] * spectra.shape[1]
    spectra = spectra.reshape(samples, 2 * piece)
    spectra = time_transform(spectra, -1.0)
    spectra = spectra * mask_factor(band_edges, samples, channels, piece)
    spectra = time_transform(spectra, 1.0)
    outgoing = spectra.reshape(lax.axis_size("tm"), samples // lax.axis_size("tm"), 1, 1, 2 * piece)
    returned = lax.all_to_all(
        lax.all_to_all(outgoing, "tm", split_axis=0, concat_axis=2, tiled=True),
        "chan",
        split_axis=1,
        concat_axis=3,
        tiled=True,
    )
    returned = returned.reshape(rows, devices, 2, piece)
    stacked = jnp.transpose(returned, (0, 2, 1, 3)).reshape(rows, 2, count)
    fanned = channel_inverse(stacked, channels)
    local = lax.all_to_all(fanned, "chan", split_axis=1, concat_axis=0, tiled=True)
    filtered = bandpass(local, taps)
    matches = gain_index[:, None] == jnp.arange(gain_table.shape[0], dtype=jnp.int32)[None, :]
    gains = jnp.sum(jnp.where(matches, gain_table[None, :], 0.0), axis=1)
    return filtered * gains[None, :]


def solution(mesh):
    in_specs = (P("tm", "chan"), P(), P(), P(), P("chan"))
    out_specs = P("tm", "chan")
    return jax.shard_map(
        per_device, mesh=mesh, in_specs=in_specs, out_specs=out_specs, check_vma=False
    )
```

profile of v0, /device:TPU:1, one launch (start us, length us, event | category | flops | bytes accessed | tf_op | source)
XLA Modules:
  0.0 1256.5 jit_solution(27895240847609910)
XLA Ops:
  0.0 5.7 all-to-all-start
  6.6 91.8 %all-to-all-done = f32[4,128,4096]{2,1,0:T(8,128)} async-done(((f32[4,128,4096]{2,1,0:T(8,128)}), f32[4,128,4096]{2,1,0:T(8,128)}, u32[]{:S(2)}, u32[]{:S(2)}) %all-to-all-start) | async-done | bytes 8388640 | tf_op jit(solution)/shard_map/all_to_all | solution.py:164
  98.4 12.2 copy.135
  110.5 11.0 reshape.450
  121.5 16.9 %convolution_bitcast_fusion.1 = f32[128,2,128,128]{3,2,0,1:T(8,128)S(1)} fusion(f32[128,128,128,1]{2,1,0,3:T(8,128)} %reshape.450, f32[128,1,128]{0,2,1:T(8,128)S(1)} %get-tuple-element.37, f32[128,1,128]{0,2,1:T(8,128)S(1)} %get-tuple-element.38), kind=kOutput, calls=%fused_computation.46 | convolution fusion | flops 6442483712 | bytes 25296896 | tf_op jit(solution)/shard_map/rba,bsg->rsga/dot_general | solution.py:50
  138.4 7.2 multiply_add_fusion.1
  145.6 18.8 %fusion.32 = f32[128,2,64,128]{3,2,0,1:T(8,128)S(1)} fusion(f32[1,128,2,64]{1,3,0,2:T(8,128)S(1)} %get-tuple-element.32, f32[1,128,2,64]{1,3,0,2:T(8,128)S(1)} %get-tuple-element.31, f32[128,1,128,128]{3,2,0,1:T(8,128)} %get-tuple-element.10, f32[128,1,128,128]{3,2,0,1:T(8,128)} %get-tuple-element.9), kind=kOutput, calls=%fused_computation.48 | convolution fusion | flops 6446678016 | bytes 25296896 | tf_op jit(solution)/shard_map/rsga,saph->rphg/dot_general | solution.py:62
  164.5 4.2 fusion.171
  168.7 5.5 copy.170
  174.2 5.4 copy.171
  179.6 4.0 pad_maximum_fusion.3
  183.6 189.3 %all_to_all.101 = f32[1,128,16384]{1,0,2:T(1,128)S(1)} all-to-all(f32[1,128,16384]{1,0,2:T(1,128)S(1)} %bitcast.164), channel_id=1, replica_groups=mesh['tm'=8,'chan'=4] {'tm'}, dimensions={2} | all-to-all | bytes 16777216 | tf_op jit(solution)/shard_map/all_to_all | solution.py:175
  372.9 12.8 %copy.205 = f32[1,128,8,2048]{1,2,3,0:T(8,128)} copy(f32[1,128,8,2048]{1,3,2,0:T(8,128)S(1)} %bitcast.165) | data formatting | bytes 16777216 | tf_op jit(solution)/shard_map/all_to_all | solution.py:175
  385.7 8.0 all-to-all-start.2
  397.8 88.3 %all-to-all-done.2 = f32[8,128,2048]{1,0,2:T(8,128)} async-done(((f32[8,128,2048]{1,0,2:T(8,128)}), f32[8,128,2048]{1,0,2:T(8,128)}, u32[]{:S(2)}, u32[]{:S(2)}) %all-to-all-start.2) | async-done | bytes 8388640 | tf_op jit(solution)/shard_map/all_to_all | solution.py:174
  486.1 9.9 copy.142
  496.0 16.8 %fusion.24 = f32[64,64,512]{2,0,1:T(8,128)S(1)} fusion(f32[64,64,512]{2,1,0:T(8,128)} %bitcast.155), kind=kOutput, calls=%fused_computation.41 | convolution fusion | flops 1610670080 | bytes 16777216 | tf_op jit(solution)/shard_map/gb,bac->gac/dot_general | solution.py:103
  516.1 13.9 %fusion.7 = f32[64,64,512]{2,0,1:T(8,128)S(1)} fusion(f32[64,64,256]{2,0,1:T(8,128)} %get-tuple-element.26, f32[64,64,256]{2,0,1:T(8,128)S(1)} %get-tuple-element.25, f32[512]{0:T(512)S(1)} %copy-done.7, f32[64,64,512]{2,1,0:T(8,128)S(1)} %bitcast.158), kind=kOutput, calls=%fused_computation.12 | convolution fusion | flops 1616961536 | bytes 25167872 | tf_op jit(solution)/shard_map/gb,bac->gac/dot_general | solution.py:102
  532.7 4.3 fusion.9
  537.0 12.6 %fusion.20 = f32[64,64,512]{2,0,1:T(8,128)S(1)} fusion(f32[64,64,512]{2,0,1:T(8,128)S(1)} %fusion.9), kind=kOutput, calls=%fused_computation.37 | convolution fusion | flops 1610670080 | bytes 16777216 | tf_op jit(solution)/shard_map/ha,gac->hgc/dot_general | solution.py:110
  549.7 4.5 fusion.168
  554.1 19.8 %fusion.11 = f32[64,64,512]{2,0,1:T(8,128)} fusion(f32[64,64,256]{2,0,1:T(8,128)} %get-tuple-element.22, f32[64,64,256]{2,0,1:T(8,128)} %get-tuple-element.21, f32[64,64,256]{2,0,1:T(8,128)} %select_multiply_fusion, f32[512]{0:T(512)S(1)} %copy-done.7, f32[64,64,512]{2,0,1:T(8,128)S(1)} %fusion.9), kind=kOutput, calls=%fused_computation.18 | convolution fusion | flops 1621155840 | bytes 29362176 | tf_op jit(solution)/shard_map/ha,gac->hgc/dot_general | solution.py:109
  573.9 11.8 fusion.82
  589.0 10.9 fusion.12
  602.6 4.3 fusion.14
  606.9 12.6 %fusion.16 = f32[64,64,512]{2,0,1:T(8,128)S(1)} fusion(f32[64,64,512]{2,0,1:T(8,128)S(1)} %fusion.14), kind=kOutput, calls=%fused_computation.33 | convolution fusion | flops 1610670080 | bytes 16777216 | tf_op jit(solution)/shard_map/ha,gac->hgc/dot_general | solution.py:110
  622.5 13.7 %fusion.15 = f32[64,64,512]{2,0,1:T(8,128)S(1)} fusion(f32[64,64,256]{2,0,1:T(8,128)} %get-tuple-element.16, f32[64,64,256]{2,0,1:T(8,128)S(1)} %get-tuple-element.15, f32[512]{0:T(512)S(1)} %copy-done.6, f32[64,64,512]{2,0,1:T(8,128)S(1)} %fusion.14), kind=kOutput, calls=%fused_computation.25 | convolution fusion | flops 1616961536 | bytes 25167872 | tf_op jit(solution)/shard_map/ha,gac->hgc/dot_general | solution.py:109
  636.2 4.9 copy.153
  641.0 185.2 %all_to_all.102 = f32[8,512,1,1,512]{4,1,3,2,0:T(8,128)S(1)} all-to-all(f32[8,512,1,1,512]{4,1,3,2,0:T(8,128)S(1)} %bitcast.166), channel_id=1, replica_groups=mesh['tm'=8,'chan'=4] {'tm'}, dimensions={0} | all-to-all | bytes 16777216 | tf_op jit(solution)/shard_map/all_to_all | solution.py:188
  826.2 8.3 copy.155
  834.5 7.4 all-to-all-start.4
  842.5 91.8 %all-to-all-done.4 = f32[1,512,8,1,512]{4,2,3,0,1:T(8,128)} async-done(((f32[1,512,8,1,512]{4,2,3,0,1:T(8,128)}), f32[1,512,8,1,512]{4,2,3,0,1:T(8,128)}, u32[]{:S(2)}, u32[]{:S(2)}) %all-to-all-start.4) | async-done | bytes 8388640 | tf_op jit(solution)/shard_map/all_to_all | solution.py:187
  934.2 10.0 copy.156
  944.2 10.4 copy.157
  954.6 8.9 reshape.457
  963.5 15.8 %convolution_bitcast_fusion = f32[128,2,128,128]{3,2,0,1:T(8,128)S(1)} fusion(f32[128,2,64,128,1]{3,2,1,0,4:T(8,128)} %reshape.457, f32[1,64,2,128]{3,1,0,2:T(8,128)S(1)} %get-tuple-element.30, f32[1,64,2,128]{3,1,0,2:T(8,128)S(1)} %get-tuple-element.29), kind=kOutput, calls=%fused_computation.45 | convolution fusion | flops 6442483712 | bytes 25296896 | tf_op jit(solution)/shard_map/rshg,shpa->rpga/dot_general | solution.py:75
  979.4 7.2 multiply_subtract_fusion
  986.7 14.3 %fusion.35 = f32[128,128,128]{2,1,0:T(8,128)} fusion(f32[128,1,128,128]{3,2,0,1:T(8,128)} %get-tuple-element.8, f32[128,1,128,128]{3,2,0,1:T(8,128)} %get-tuple-element.7, f32[1,128,128]{1,2,0:T(8,128)S(1)} %get-tuple-element.45, f32[1,128,128]{1,2,0:T(8,128)S(1)} %get-tuple-element.46), kind=kOutput, calls=%fused_computation.49 | convolution fusion | flops 6446678016 | bytes 25296896 | tf_op jit(solution)/shard_map/rsga,sgb->rba/dot_general | solution.py:84
  1000.9 9.9 all_to_all.91
  1010.9 8.2 copy.160
  1019.1 95.7 %all_to_all.103 = f32[128,4,4096]{2,0,1:T(8,128)S(1)} all-to-all(f32[128,4,4096]{2,0,1:T(8,128)S(1)} %copy.160), channel_id=1, replica_groups=mesh['tm'=8,'chan'=4] {'chan'}, dimensions={1} | all-to-all | bytes 16777216 | tf_op jit(solution)/shard_map/all_to_all | solution.py:197
  1114.8 3.4 copy-done
  1127.1 15.4 %fusion.60 = f32[4,4096,128]{1,2,0:T(8,128)} fusion(f32[128,255]{1,0:T(8,128)S(1)} %reshape.446, f32[128,4,4096]{2,0,1:T(8,128)} %copy-done), kind=kOutput, calls=%fused_computation.88 | convolution fusion | flops 3221225472 | bytes 16842752 | tf_op jit(solution)/shard_map/ab,jac->jbc/dot_general | solution.py:151
  1142.5 70.2 %collective-permute-done = f32[128,4096]{1,0:T(8,128)S(1)} collective-permute-done((f32[128,4096]{1,0:T(8,128)}, f32[128,4096]{1,0:T(8,128)S(1)}, u32[]{:S(2)}, u32[]{:S(2)}) %collective-permute-start) | collective-permute-done | bytes 2097184 | tf_op jit(solution)/shard_map/ppermute | solution.py:19
  1212.7 8.7 pad_maximum_fusion.1
  1221.3 13.0 %fusion.61 = f32[4,4096,128]{1,2,0:T(8,128)} fusion(f32[4,128,4096]{2,1,0:T(8,128)S(1)} %bitcast.161, f32[128,255]{1,0:T(8,128)S(1)} %reshape.445), kind=kOutput, calls=%fused_computation.90 | convolution fusion | flops 3221225472 | bytes 16842752 | tf_op jit(solution)/shard_map/ab,jac->jbc/dot_general | solution.py:151
  1234.4 17.5 %add_add_fusion = f32[4,4096,128]{1,2,0:T(8,128)S(1)} fusion(f32[4,4096,128]{1,2,0:T(8,128)} %fusion.61, f32[4,4096,128]{1,2,0:T(8,128)} %fusion.60, f32[4,128,4096]{2,1,0:T(8,128)} %bitcast.163, f32[128,255]{1,0:T(8,128)S(1)} %reshape.447), kind=kOutput, calls=%fused_computation.28 | convolution fusion | flops 3225419776 | bytes 33619968 | tf_op jit(solution)/shard_map/ab,jac->jbc/dot_general | solution.py:151
  1252.0 4.3 bitcast_multiply_fusion
  (81 shorter events, 29.3 us)
Async XLA Ops:
  0.0 98.3 %all-to-all-start = ((f32[4,128,4096]{2,1,0:T(8,128)}), f32[4,128,4096]{2,1,0:T(8,128)}, u32[]{:S(2)}, u32[]{:S(2)}) async-start(f32[4,128,4096]{2,1,0:T(8,128)} %bitcast.171), calls=%async_computation | async-start | bytes 16777216 | tf_op jit(solution)/shard_map/all_to_all | solution.py:164
  6.5 131.9 %copy-start.1 = (f32[128,128]{1,0:T(8,128)}, f32[128,128]{1,0:T(8,128)S(1)}, u32[]{:S(2)}) copy-start(f32[128,128]{1,0:T(8,128)S(1)} %get-tuple-element.39) | copy-start | bytes 196612
  6.5 131.9 %copy-start.3 = (f32[128,128]{1,0:T(8,128)}, f32[128,128]{1,0:T(8,128)S(1)}, u32[]{:S(2)}) copy-start(f32[128,128]{1,0:T(8,128)S(1)} %get-tuple-element.40) | copy-start | bytes 196612
  385.7 8.5 copy-start.5
  385.7 100.4 %all-to-all-start.2 = ((f32[8,128,2048]{1,0,2:T(8,128)}), f32[8,128,2048]{1,0,2:T(8,128)}, u32[]{:S(2)}, u32[]{:S(2)}) async-start(f32[8,128,2048]{1,0,2:T(8,128)} %bitcast.162), calls=%async_computation.2 | async-start | bytes 16777216 | tf_op jit(solution)/shard_map/all_to_all | solution.py:174
  496.0 19.6 %slice-start = ((s8[8388608]{0:T(1024)(128)(4,1)}), s8[4194304]{0:T(1024)(128)(4,1)S(1)}, s32[]{:S(2)}) async-start(s8[8388608]{0:T(1024)(128)(4,1)} %bitcast.156), calls=%async_computation.6 | async-start | bytes 8388608
  512.8 3.3 slice-start.1
  512.8 3.3 copy-start.7
  573.9 14.6 %slice-start.2 = ((s8[8388608]{0:T(1024)(128)(4,1)}), s8[4194304]{0:T(1024)(128)(4,1)S(1)}, s32[]{:S(2)}) async-start(s8[8388608]{0:T(1024)(128)(4,1)} %bitcast.159), calls=%async_computation.8 | async-start | bytes 8388608
  585.7 3.3 slice-start.3
  585.7 3.3 copy-start.6
  834.5 99.8 %all-to-all-start.4 = ((f32[1,512,8,1,512]{4,2,3,0,1:T(8,128)}), f32[1,512,8,1,512]{4,2,3,0,1:T(8,128)}, u32[]{:S(2)}, u32[]{:S(2)}) async-start(f32[1,512,8,1,512]{4,2,3,0,1:T(8,128)} %copy.155), calls=%async_computation.4 | async-start | bytes 16777216 | tf_op jit(solution)/shard_map/all_to_all | solution.py:187
  963.5 15.8 %copy-start.2 = (f32[128,128]{1,0:T(8,128)S(1)}, f32[128,128]{1,0:T(8,128)}, u32[]{:S(2)}) copy-start(f32[128,128]{1,0:T(8,128)} %copy-done.1) | copy-start | bytes 196612
  963.5 15.9 %copy-start.4 = (f32[128,128]{1,0:T(8,128)S(1)}, f32[128,128]{1,0:T(8,128)}, u32[]{:S(2)}) copy-start(f32[128,128]{1,0:T(8,128)} %copy-done.3) | copy-start | bytes 196612
  1114.8 3.4 copy-start
  1114.8 10.2 copy-start.9
  1114.8 12.1 copy-start.8
  1114.8 12.1 copy-start.10
  1120.5 92.2 %collective-permute-start = (f32[128,4096]{1,0:T(8,128)}, f32[128,4096]{1,0:T(8,128)S(1)}, u32[]{:S(2)}, u32[]{:S(2)}) collective-permute-start(f32[128,4096]{1,0:T(8,128)} %get-tuple-element.14), channel_id=1, source_target_pairs={{0,4},{4,8},{8,12},{12,16},{16,20},{20,24},{24,28},{1,5},{5,9},{9,... | collective-permute-start | bytes 6291464 | tf_op jit(solution)/shard_map/ppermute | solution.py:19
  1123.7 89.0 %collective-permute-start.1 = (f32[128,4096]{1,0:T(8,128)}, f32[128,4096]{1,0:T(8,128)}, u32[]{:S(2)}, u32[]{:S(2)}) collective-permute-start(f32[128,4096]{1,0:T(8,128)} %get-tuple-element.13), channel_id=1, source_target_pairs={{4,0},{8,4},{12,8},{16,12},{20,16},{24,20},{28,24},{5,1},{9,5},{13... | collective-permute-start | bytes 6291464 | tf_op jit(solution)/shard_map/ppermute | solution.py:21
where the time goes:
time: 1270 us; the launch traced here: 1260 us
  blocking collectives  470 us (37%)
  waiting for transfers between devices  342 us (27%)
  matrix products  224 us (18%)
  local copies, waits for them, and re-layouts  149 us (12%)
  other arithmetic  45.3 us (4%)
  starting transfers between devices  25.6 us (2%)
    all_to_all x1, blocking collectives, per_device(): lax.all_to_all(packed, 'tm', split_axis=2, concat_axis=0, tiled=True)  189 us
    all_to_all x1, blocking collectives, per_device(): lax.all_to_all(outgoing, 'tm', split_axis=0, concat_axis=2, tiled=True)  185 us
    all_to_all x1, blocking collectives, per_device(): lax.all_to_all(fanned, 'chan', split_axis=1, concat_axis=0, tiled=True)  95.7 us
    all_to_all x1, waiting for transfers between devices, per_device(): lax.all_to_all(traces, 'chan', split_axis=0, concat_axis=1, tiled=True)  91.8 us
    all_to_all x1, waiting for transfers between devices, per_device(): lax.all_to_all(lax.all_to_all(outgoing, 'tm', split_axis=0, concat_axis=2...  91.8 us
    all_to_all x1, waiting for transfers between devices, per_device(): lax.all_to_all(lax.all_to_all(packed, 'tm', split_axis=2, concat_axis=0,...  88.3 us
    ppermute x1, waiting for transfers between devices, extended(): lax.ppermute(tail, axis, [(i, (i + 1) % count) for i in range(ends)])  70.2 us
    dot_general x3, matrix products, apply_tiles(): jnp.einsum('ab,jac->jbc', kernels[shift], blocks[shift:shift + tiles], pr...  46 us
  transfers between devices with their start and end apart: 5, of which 4 were waited for; matrix products, arithmetic and copies ran while one was open for 2% of the time, Pallas kernels for 0%

commit v1 on v0

v1 whole, which is shorter than its diff:
```python
import functools
import math

import jax
import jax.numpy as jnp
import ml_dtypes
import numpy as np
from jax import lax
from jax.experimental import pallas as pl
from jax.experimental.pallas import tpu as pltpu
from jax.sharding import PartitionSpec as P

WIDE = 256
LANES = 128
AXES = ("tm", "chan")
F32 = jnp.float32


def halves(table):
    table = np.asarray(table, np.float32)
    high = table.astype(ml_dtypes.bfloat16)
    low = (table - high.astype(np.float32)).astype(ml_dtypes.bfloat16)
    return np.stack([high, low])


def turn(product, period):
    theta = (product % period) * (2.0 * math.pi / period)
    return np.cos(theta), np.sin(theta)


def channel_tables(channels):
    radix = channels // WIDE
    a = np.arange(WIDE)
    cos, sin = turn(a[:, None] * a[None, :], WIDE)
    sign = np.where(a < WIDE // 2, 1.0, -1.0)
    table = np.block([[cos, -sin * sign], [sin, cos * sign]])
    low = np.arange(WIDE // 2)
    cos_0, sin_0 = turn(a[:, None] * low[None, :], WIDE)
    cos_m, sin_m = turn(a[:, None] * (radix // 2 + radix * low)[None, :], channels)
    none = np.zeros_like(cos_0)
    first = np.block([[cos_0, none, -sin_0, none], [none, cos_m, none, -sin_m]])
    cos_t, sin_t = turn(np.arange(radix // 2)[:, None] * a[None, :], channels)
    return table, first, cos_t.astype(np.float32), sin_t.astype(np.float32)


def wave_order(channels):
    radix = channels // WIDE
    h = np.arange(WIDE)
    low = np.arange(WIDE // 2)
    rows = [np.concatenate([radix * low, radix // 2 + radix * low])]
    for g in range(1, radix // 2):
        wave = g + radix * h
        rows.append(np.where(h < WIDE // 2, wave, channels - wave))
    return np.concatenate(rows).astype(np.int32)


def real_forward(x):
    n = len(x)
    if n == 2:
        return [(x[0] + x[1], None), (x[0] - x[1], None)]
    even, odd = real_forward(x[0::2]), real_forward(x[1::2])
    out = [None] * (n // 2 + 1)
    out[0] = (even[0][0] + odd[0][0], None)
    out[n // 2] = (even[0][0] - odd[0][0], None)
    out[n // 4] = (even[n // 4][0], -odd[n // 4][0])
    for k in range(1, n // 4):
        c, s = math.cos(2 * math.pi * k / n), math.sin(2 * math.pi * k / n)
        er, ei = even[k]
        o_r, o_i = odd[k]
        wr, wi = o_r * c + o_i * s, o_i * c - o_r * s
        out[k] = (er + wr, ei + wi)
        out[n // 2 - k] = (er - wr, wi - ei)
    return out


def real_inverse(v):
    n = 2 * (len(v) - 1)
    if n == 2:
        return [v[0][0] + v[1][0], v[0][0] - v[1][0]]
    q = n // 4
    even, odd = [None] * (q + 1), [None] * (q + 1)
    even[0] = (v[0][0] + v[n // 2][0], None)
    odd[0] = (v[0][0] - v[n // 2][0], None)
    even[q] = (v[q][0], None)
    odd[q] = (-v[q][1], None)
    for g in range(1, q):
        c, s = math.cos(2 * math.pi * g / n), math.sin(2 * math.pi * g / n)
        ar, ai = v[g]
        br, bi = v[n // 2 - g]
        even[g] = (ar + br, ai - bi)
        dr, di = ar - br, ai + bi
        odd[g] = (dr * c - di * s, di * c + dr * s)
    out = [None] * n
    out[0::2], out[1::2] = real_inverse(even), real_inverse(odd)
    return out


def complex_short(x, direction):
    n = len(x)
    if n == 1:
        return x
    even, odd = complex_short(x[0::2], direction), complex_short(x[1::2], direction)
    out = [None] * n
    for k in range(n // 2):
        o_r, o_i = odd[k]
        if k == 0:
            wr, wi = o_r, o_i
        elif 4 * k == n:
            wr, wi = -direction * o_i, direction * o_r
        else:
            c = math.cos(2 * math.pi * k / n)
            s = direction * math.sin(2 * math.pi * k / n)
            wr, wi = o_r * c - o_i * s, o_i * c + o_r * s
        er, ei = even[k]
        out[k] = (er + wr, ei + wi)
        out[k + n // 2] = (er - wr, ei - wi)
    return out


def split(x):
    high = x.astype(jnp.bfloat16)
    return high, (x - high.astype(F32)).astype(jnp.bfloat16)


def dot(a, b):
    return jnp.dot(a, b, preferred_element_type=F32)


def dot_right(x, table):
    high, low = split(x)
    return dot(high, table[0]) + (dot(low, table[0]) + dot(high, table[1]))


def dot_left(table, x):
    high, low = split(x)
    return dot(table[0], high) + (dot(table[0], low) + dot(table[1], high))


def forward_kernel(x_ref, table_ref, first_ref, cos_ref, sin_ref, out_ref, held):
    owners, rows, width = x_ref.shape
    slots = held.shape[0]
    per = width // WIDE

    @pl.loop(0, rows // 8)
    def _(tile):
        at = pl.ds(pl.multiple_of(tile * 8, 8), 8)
        for lane in range(0, WIDE, LANES):
            x = [
                x_ref[j, at, pl.ds(b * WIDE + lane, LANES)]
                for j in range(owners)
                for b in range(per)
            ]
            g = real_forward(x)
            held[0, at, pl.ds(lane, LANES)] = g[0][0]
            held[0, at, pl.ds(WIDE + lane, LANES)] = g[slots][0]
            for k in range(1, slots):
                c = cos_ref[pl.ds(k, 1), pl.ds(lane, LANES)]
                s = sin_ref[pl.ds(k, 1), pl.ds(lane, LANES)]
                re, im = g[k]
                held[k, at, pl.ds(lane, LANES)] = re * c + im * s
                held[k, at, pl.ds(WIDE + lane, LANES)] = im * c - re * s

    group = min(8, slots)

    @pl.loop(0, slots // group)
    def _(step):
        at = pl.ds(step * group, group)
        x = held[at].reshape(group * rows, 2 * WIDE)
        y = dot_right(x, table_ref).reshape(group, rows, 2 * WIDE)
        out_ref[at, 0] = y[:, :, :WIDE]
        out_ref[at, 1] = y[:, :, WIDE:]

    y = dot_right(held[0], first_ref)
    out_ref[0, 0] = y[:, :WIDE]
    out_ref[0, 1] = y[:, WIDE:]


def inverse_kernel(x_ref, table_ref, first_ref, cos_ref, sin_ref, gain_ref, out_ref, held):
    owners, rows, width = out_ref.shape
    slots = held.shape[0]
    per = width // WIDE
    group = min(8, slots)

    @pl.loop(0, slots // group)
    def _(step):
        at = pl.ds(step * group, group)
        x = jnp.concatenate([x_ref[at, 0], x_ref[at, 1]], axis=-1)
        y = dot_right(x.reshape(group * rows, 2 * WIDE), table_ref)
        held[at] = y.reshape(group, rows, 2 * WIDE)

    held[0] = dot_right(jnp.concatenate([x_ref[0, 0], x_ref[0, 1]], axis=-1), first_ref)

    @pl.loop(0, rows // 8)
    def _(tile):
        at = pl.ds(pl.multiple_of(tile * 8, 8), 8)
        for lane in range(0, WIDE, LANES):
            v = [(held[0, at, pl.ds(lane, LANES)], None)]
            for k in range(1, slots):
                c = cos_ref[pl.ds(k, 1), pl.ds(lane, LANES)]
                s = sin_ref[pl.ds(k, 1), pl.ds(lane, LANES)]
                re = held[k, at, pl.ds(lane, LANES)]
                im = held[k, at, pl.ds(WIDE + lane, LANES)]
                v.append((re * c - im * s, im * c + re * s))
            v.append((held[0, at, pl.ds(WIDE + lane, LANES)], None))
            y = real_inverse(v)
            for j in range(owners):
                for b in range(per):
                    place = pl.ds(b * WIDE + lane, LANES)
                    gain = gain_ref[pl.ds(j, 1), place]
                    out_ref[j, at, place] = y[j * per + b] * gain


def whole(shape):
    return pl.BlockSpec(shape, lambda i: (0,) * len(shape))


def params():
    return pltpu.CompilerParams(vmem_limit_bytes=56 * 2**20)


def channel_forward(x):
    owners, rows, width = x.shape
    channels = owners * width
    slots = channels // WIDE // 2
    block = min(32, rows)
    table, first, cos, sin = channel_tables(channels)
    tables = [jnp.asarray(halves(table)), jnp.asarray(halves(first)), jnp.asarray(cos), jnp.asarray(sin)]
    return pl.pallas_call(
        forward_kernel,
        grid=(rows // block,),
        in_specs=[pl.BlockSpec((owners, block, width), lambda i: (0, i, 0))]
        + [whole(t.shape) for t in tables],
        out_specs=pl.BlockSpec((slots, 2, block, WIDE), lambda i: (0, 0, i, 0)),
        out_shape=jax.ShapeDtypeStruct((slots, 2, rows, WIDE), F32),
        scratch_shapes=[pltpu.VMEM((slots, block, 2 * WIDE), F32)],
        compiler_params=params(),
        name="channel_forward",
    )(x, *tables)


def channel_inverse(x, gains, owners):
    slots, _, rows, _ = x.shape
    channels = 2 * slots * WIDE
    width = channels // owners
    block = min(32, rows)
    table, first, cos, sin = channel_tables(channels)
    tables = [jnp.asarray(halves(table.T)), jnp.asarray(halves(first.T)), jnp.asarray(cos), jnp.asarray(sin), gains]
    return pl.pallas_call(
        inverse_kernel,
        grid=(rows // block,),
        in_specs=[pl.BlockSpec((slots, 2, block, WIDE), lambda i: (0, 0, i, 0))]
        + [whole(t.shape) for t in tables],
        out_specs=pl.BlockSpec((owners, block, width), lambda i: (0, i, 0)),
        out_shape=jax.ShapeDtypeStruct((owners, rows, width), F32),
        scratch_shapes=[pltpu.VMEM((slots, block, 2 * WIDE), F32)],
        compiler_params=params(),
        name="channel_inverse",
    )(x, *tables)


def time_kernel(x_ref, table_ref, cos_ref, sin_ref, factor_ref, fir_ref, out_ref, held, line):
    devices, _, rows, lanes = x_ref.shape
    radix = held.shape[1]
    per = WIDE // rows

    for part in range(per):
        @pl.loop(0, rows // 8)
        def _(tile):
            at = pl.ds(pl.multiple_of(tile * 8, 8), 8)
            to = pl.ds(pl.multiple_of(part * rows + tile * 8, 8), 8)
            x = [(x_ref[b * per + part, 0, at], x_ref[b * per + part, 1, at]) for b in range(radix)]
            y = complex_short(x, -1.0)
            for g in range(radix):
                re, im = y[g]
                c, s = cos_ref[g, to], sin_ref[g, to]
                held[0, g, to] = re * c + im * s
                held[1, g, to] = im * c - re * s

    @pl.loop(0, radix)
    def _(g):
        y = dot_left(table_ref, jnp.concatenate([held[0, g], held[1, g]], axis=1))
        factor = factor_ref[g]
        re = (y[:WIDE, :lanes] + y[WIDE:, lanes:]) * factor
        im = (y[:WIDE, lanes:] - y[WIDE:, :lanes]) * factor
        y = dot_left(table_ref, jnp.concatenate([re, im], axis=1))
        re = y[:WIDE, :lanes] - y[WIDE:, lanes:]
        im = y[:WIDE, lanes:] + y[WIDE:, :lanes]
        c, s = cos_ref[g], sin_ref[g]
        held[0, g] = re * c - im * s
        held[1, g] = im * c + re * s

    edge = line.shape[1] - LANES
    for part in range(2):
        line[part, :LANES] = jnp.zeros((LANES, lanes), F32)
        line[part, edge:] = jnp.zeros((LANES, lanes), F32)

    @pl.loop(0, WIDE // 8)
    def _(tile):
        at = pl.ds(pl.multiple_of(tile * 8, 8), 8)
        y = complex_short([(held[0, g, at], held[1, g, at]) for g in range(radix)], 1.0)
        for b in range(radix):
            to = pl.ds(pl.multiple_of(LANES + b * WIDE + tile * 8, 8), 8)
            line[0, to] = y[b][0]
            line[1, to] = y[b][1]

    @pl.loop(0, radix)
    def _(b):
        at = pl.ds(pl.multiple_of(b * WIDE, WIDE), 2 * WIDE)
        y = dot_left(fir_ref, jnp.concatenate([line[0, at], line[1, at]], axis=1))
        to = pl.ds(b * per, per)
        out_ref[to, 0] = y[:, :lanes].reshape(per, rows, lanes)
        out_ref[to, 1] = y[:, lanes:].reshape(per, rows, lanes)


def fir_table(taps):
    count = taps.shape[0]
    shift = LANES - (count - 1) // 2
    period = 2 * WIDE + 1
    row = jnp.pad(taps, (shift, period - count - shift))
    table = jnp.tile(row, WIDE)[: WIDE * 2 * WIDE].reshape(WIDE, 2 * WIDE)
    high = lax.reduce_precision(table, 8, 7)
    return jnp.stack([high, table - high]).astype(jnp.bfloat16)


def time_stage(x, factor, taps):
    devices, _, rows, piece = x.shape
    samples = devices * rows
    radix = samples // WIDE
    a = np.arange(WIDE)
    cos, sin = turn(a[:, None] * a[None, :], WIDE)
    table = jnp.asarray(halves(np.concatenate([cos, sin], axis=0)))
    cos_t, sin_t = turn(np.arange(radix)[:, None] * a[None, :], samples)
    turns = [
        jnp.broadcast_to(jnp.asarray(t.astype(np.float32))[:, :, None], (radix, WIDE, LANES))
        for t in (cos_t, sin_t)
    ]
    fir = fir_table(taps)
    block = pl.BlockSpec((devices, 2, rows, LANES), lambda i: (0, 0, 0, i))
    return pl.pallas_call(
        time_kernel,
        grid=(piece // LANES,),
        in_specs=[
            block,
            whole(table.shape),
            whole(turns[0].shape),
            whole(turns[1].shape),
            pl.BlockSpec((radix, WIDE, LANES), lambda i: (0, 0, i)),
            whole(fir.shape),
        ],
        out_specs=block,
        out_shape=jax.ShapeDtypeStruct(x.shape, F32),
        scratch_shapes=[
            pltpu.VMEM((2, radix, WIDE, LANES), F32),
            pltpu.VMEM((2, samples + 2 * LANES, LANES), F32),
        ],
        compiler_params=params(),
        name="time_stage",
    )(x, table, *turns, factor, fir)


def mask_factor(band_edges, channels, piece, width):
    samples = band_edges.shape[1]
    owner = lax.axis_index("tm") * lax.axis_size("chan") + lax.axis_index("chan")
    order = jnp.asarray(wave_order(channels))
    wave = lax.dynamic_slice_in_dim(order, owner * piece, piece)
    wave = jnp.pad(wave, (0, width - piece))[None, None, :]
    edges = band_edges.reshape(2, WIDE, samples // WIDE).transpose(0, 2, 1)[:, :, :, None]
    kept = (wave >= edges[0]) & (wave <= edges[1])
    weight = jnp.where(wave == 0, 1.0, 2.0).astype(F32)
    return jnp.where(kept, weight, 0.0) / float(samples * channels)


def regroup(x, devices):
    slots, _, rows, _ = x.shape
    share = devices // slots
    if share == 1:
        return x
    x = x.reshape(slots, 2, rows, share, WIDE // share).transpose(0, 3, 1, 2, 4)
    return x.reshape(devices, 2, rows, WIDE // share)


def ungroup(x, slots):
    devices, _, rows, piece = x.shape
    share = devices // slots
    if share == 1:
        return x
    x = x.reshape(slots, share, 2, rows, piece).transpose(0, 2, 3, 1, 4)
    return x.reshape(slots, 2, rows, WIDE)


def exchange(x, axes):
    return lax.all_to_all(x, axes, split_axis=0, concat_axis=0, tiled=True)


def per_device(traces, band_edges, taps, gain_table, gain_index):
    owners = lax.axis_size("chan")
    devices = lax.axis_size("tm") * owners
    length, width = traces.shape
    channels = owners * width
    slots = channels // WIDE // 2
    piece = channels // 2 // devices
    padded = max(piece, LANES)
    matches = gain_index[:, None] == jnp.arange(gain_table.shape[0], dtype=jnp.int32)[None, :]
    gains = jnp.sum(jnp.where(matches, gain_table[None, :], 0.0), axis=1)
    gains = lax.all_gather(gains, "chan")
    factor = mask_factor(band_edges, channels, piece, padded)

    gathered = exchange(traces.reshape(owners, length // owners, width), "chan")
    spectra = exchange(regroup(channel_forward(gathered), devices), AXES)
    if padded > piece:
        spectra = jnp.pad(spectra, ((0, 0), (0, 0), (0, 0), (0, padded - piece)))
    spectra = time_stage(spectra, factor, taps)
    if padded > piece:
        spectra = spectra[..., :piece]
    returned = ungroup(exchange(spectra, AXES), slots)
    local = exchange(channel_inverse(returned, gains, owners), "chan")
    return local.reshape(length, width)


def solution(mesh):
    in_specs = (P("tm", "chan"), P(), P(), P(), P("chan"))
    out_specs = P("tm", "chan")
    return jax.shard_map(
        per_device, mesh=mesh, in_specs=in_specs, out_specs=out_specs, check_vma=False
    )
```

time: 1270 us -> 687 us (0.54)
  blocking collectives: 470 us -> 245 us
  matrix products: 224 us -> 0 us
  local copies, waits for them, and re-layouts: 149 us -> 9.7 us
  Pallas kernels: 0 us -> 96.2 us
  other arithmetic: 45.3 us -> 4.95 us
  waiting for transfers between devices: 342 us -> 314 us
    all_to_all x3 -> x2, blocking collectives: 470 us -> 197 us  [exchange(): return lax.all_to_all(x, axes, split_axis=0, concat_axis=0, tiled=True)]
    dot_general x15 -> x0, matrix products: 224 us -> none  [the longest x3 46 us: apply_tiles(): jnp.einsum('ab,jac->jbc', kernels[shift], blocks[shift:shift + tiles], pr...]
    pallas_call x0 -> x3, Pallas kernels: none -> 96.2 us  [the longest x1 59.6 us: time_stage(): pl.pallas_call(time_kernel, grid=(piece // LANES,), in_specs=[block, whol...]
    all_to_all x7 -> x0, local copies, waits for them, and re-layouts: 71.3 us -> none  [the longest x2 18.2 us: per_device(): lax.all_to_all(fanned, 'chan', split_axis=1, concat_axis=0, tiled=True)]
    ppermute x2 -> x0, waiting for transfers between devices: 70.2 us -> none  [the longest x1 70.2 us: extended(): lax.ppermute(tail, axis, [(i, (i + 1) % count) for i in range(ends)])]
    all_gather x0 -> x1, blocking collectives: none -> 47.7 us  [per_device(): gains = lax.all_gather(gains, 'chan')]
    all_to_all x3 -> x2, waiting for transfers between devices: 272 us -> 314 us  [exchange(): return lax.all_to_all(x, axes, split_axis=0, concat_axis=0, tiled=True)]
    slice x17 -> x1, local copies, waits for them, and re-layouts: 25.5 us -> 0.04 us  [fir_table(): table = jnp.tile(row, WIDE)[:WIDE * 2 * WIDE].reshape(WIDE, 2 * WIDE)]
  transfers between devices with their start and end apart: 5 -> 2, of which waited for: 4 -> 2; matrix products, arithmetic and copies ran while one was open for 2% -> 1% of each run, Pallas kernels for 0% -> 0%
where the time goes in v1:
time: 687 us; the launch traced here: 685 us
  waiting for transfers between devices  314 us (46%)
  blocking collectives  245 us (36%)
  Pallas kernels  96.2 us (14%)
  starting transfers between devices  14.5 us (2%)
  local copies, waits for them, and re-layouts  9.7 us (1%)
    all_to_all x2, waiting for transfers between devices, exchange(): return lax.all_to_all(x, axes, split_axis=0, concat_axis=0, tiled=True)  314 us
    all_to_all x2, blocking collectives, exchange(): return lax.all_to_all(x, axes, split_axis=0, concat_axis=0, tiled=True)  197 us
    pallas_call x1, Pallas kernels, time_stage(): pl.pallas_call(time_kernel, grid=(piece // LANES,), in_specs=[block, whol...  59.6 us
    all_gather x1, blocking collectives, per_device(): gains = lax.all_gather(gains, 'chan')  47.7 us
    pallas_call x1, Pallas kernels, channel_inverse(): pl.pallas_call(inverse_kernel, grid=(rows // block,), in_specs=[pl.BlockS...  18.7 us
    pallas_call x1, Pallas kernels, channel_forward(): pl.pallas_call(forward_kernel, grid=(rows // block,), in_specs=[pl.BlockS...  17.9 us
    all_to_all x2, starting transfers between devices, exchange(): return lax.all_to_all(x, axes, split_axis=0, concat_axis=0, tiled=True)  14.5 us
  transfers between devices with their start and end apart: 2, of which 2 were waited for; matrix products, arithmetic and copies ran while one was open for 1% of the time, Pallas kernels for 0%

profile of v1, /device:TPU:1, one launch (start us, length us, event | category | flops | bytes accessed | tf_op | source)
XLA Modules:
  0.0 684.7 jit_solution(3531835834599090995)
XLA Ops:
  0.0 100.3 %all_to_all.20.x_ref = f32[4,128,4096]{2,1,0:T(8,128)} all-to-all(f32[4,128,4096]{2,1,0:T(8,128)} %bitcast.8), channel_id=1, replica_groups=mesh['tm'=8,'chan'=4] {'chan'}, dimensions={0} | all-to-all | bytes 16777216 | tf_op jit(solution)/shard_map/all_to_all | solution.py:392
  100.3 17.9 %channel_forward.1 = f32[32,2,128,256]{3,2,1,0:T(8,128)} custom-call(f32[4,128,4096]{2,1,0:T(8,128)} %all_to_all.20.x_ref, bf16[2,512,512]{2,1,0:T(8,128)(2,1)} %constant.49.clone.table_ref, bf16[2,512,512]{2,1,0:T(8,128)(2,1)} %constant.50.clone.first_ref, f32[32,256]{1,0:T(8,128)} %constant.51.clone.cos_ref, f32[32,256]{1,0:T(8,128)} %constant.52.clone.sin_ref), custom_call_target="tpu_custom_call" | custom-call | tf_op jit(solution)/shard_map/channel_forward/pallas_call | solution.py:228
  118.1 0.0 copy-start
  118.1 0.0 copy-start.4
  118.1 6.5 all-to-all-start.1
  124.7 0.0 copy-done
  124.7 0.1 reshape.51
  124.9 0.1 copy.23
  124.9 0.1 copy.24
  125.0 0.0 copy-done.4
  125.0 0.1 pad.4
  125.1 0.5 tile.10
  125.6 0.0 copy-start.2
  125.7 0.1 reshape.52
  125.8 0.8 dynamic_slice.3
  126.5 0.8 compare_select_fusion
  127.3 0.0 copy-start.1
  127.3 0.1 reduce-precision_convert_fusion
  127.4 0.9 pad_maximum_fusion.fir_ref
  128.2 3.0 select_multiply_fusion.factor_ref
  131.3 178.1 %all-to-all-done.1.x_ref = f32[32,2,128,256]{3,2,1,0:T(8,128)} async-done(((f32[32,2,128,256]{3,2,1,0:T(8,128)}), f32[32,2,128,256]{3,2,1,0:T(8,128)}, u32[]{:S(2)}, u32[]{:S(2)}) %all-to-all-start.1) | async-done | bytes 8388640 | tf_op jit(solution)/shard_map/all_to_all | solution.py:392
  309.4 0.0 copy-done.2
  309.4 1.9 broadcast_in_dim.49.cos_ref
  311.3 0.0 copy-done.1
  311.3 1.9 broadcast_in_dim.50.sin_ref
  313.2 59.6 %time_stage.1 = f32[32,2,128,256]{3,2,1,0:T(8,128)} custom-call(f32[32,2,128,256]{3,2,1,0:T(8,128)} %all-to-all-done.1.x_ref, bf16[2,512,256]{2,1,0:T(8,128)(2,1)} %constant.53.clone.table_ref, f32[16,256,128]{2,1,0:T(8,128)} %broadcast_in_dim.49.cos_ref, f32[16,256,128]{2,1,0:T(8,128)} %broadcast_in_dim.50.sin_ref, ...), custom_call_target="tpu_custom_call" | custom-call | tf_op jit(solution)/shard_map/time_stage/pallas_call | solution.py:339
  372.8 0.0 copy-start.3
  372.8 0.0 copy-start.5
  372.8 8.0 %all-to-all-start.2 = ((f32[32,2,128,256]{3,2,1,0:T(8,128)}), f32[32,2,128,256]{3,2,1,0:T(8,128)}, u32[]{:S(2)}, u32[]{:S(2)}) async-start(f32[32,2,128,256]{3,2,1,0:T(8,128)} %time_stage.1), calls=%async_computation.2 | async-start | bytes 16777216 | tf_op jit(solution)/shard_map/all_to_all | solution.py:392
  380.8 0.0 copy-done.3
  380.8 0.0 copy-done.5
  380.8 0.2 select_reduce_fusion
  381.1 47.7 %all-gather = f32[16384]{0:T(1024)S(1)} all-gather(f32[4096]{0:T(1024)S(1)} %select_reduce_fusion), channel_id=2, replica_groups=mesh['tm'=8,'chan'=4] {'chan'}, dimensions={0}, use_global_device_ids=true | all-gather | bytes 81920 | tf_op jit(solution)/shard_map/all_gather | solution.py:405
  428.8 0.6 reshape.54.gain_ref
  429.4 136.1 %all-to-all-done.2.x_ref = f32[32,2,128,256]{3,2,1,0:T(8,128)} async-done(((f32[32,2,128,256]{3,2,1,0:T(8,128)}), f32[32,2,128,256]{3,2,1,0:T(8,128)}, u32[]{:S(2)}, u32[]{:S(2)}) %all-to-all-start.2) | async-done | bytes 8388640 | tf_op jit(solution)/shard_map/all_to_all | solution.py:392
  565.6 18.7 %channel_inverse.1 = f32[4,128,4096]{2,1,0:T(8,128)} custom-call(f32[32,2,128,256]{3,2,1,0:T(8,128)} %all-to-all-done.2.x_ref, bf16[2,512,512]{2,1,0:T(8,128)(2,1)} %constant.56.clone.table_ref, bf16[2,512,512]{2,1,0:T(8,128)(2,1)} %constant.57.clone.first_ref, f32[32,256]{1,0:T(8,128)} %constant.51.clone.cos_ref, f32[32,256]{1,0:T(8,128)} %constant.52.clone.sin_ref, ...), custom_call_target="tpu_custom_call" | custom-call | tf_op jit(solution)/shard_map/channel_inverse/pallas_call | solution.py:248
  584.3 97.1 %all_to_all.21 = f32[4,128,4096]{2,1,0:T(8,128)S(1)} all-to-all(f32[4,128,4096]{2,1,0:T(8,128)} %channel_inverse.1), channel_id=1, replica_groups=mesh['tm'=8,'chan'=4] {'chan'}, dimensions={0} | all-to-all | bytes 16777216 | tf_op jit(solution)/shard_map/all_to_all | solution.py:392
  681.3 3.4 copy.26
  (3 shorter events, 0.1 us)
Async XLA Ops:
  118.1 6.6 copy-start
  118.1 6.9 %copy-start.4 = (f32[255]{0:T(256)S(1)}, f32[255]{0:T(256)}, u32[]{:S(2)}) copy-start(f32[255]{0:T(256)} %param.19) | copy-start | bytes 3064
  118.1 191.3 %all-to-all-start.1 = ((f32[32,2,128,256]{3,2,1,0:T(8,128)}), f32[32,2,128,256]{3,2,1,0:T(8,128)}, u32[]{:S(2)}, u32[]{:S(2)}) async-start(f32[32,2,128,256]{3,2,1,0:T(8,128)} %channel_forward.1), calls=%async_computation.1 | async-start | bytes 16777216 | tf_op jit(solution)/shard_map/all_to_all | solution.py:392
  125.6 183.8 %copy-start.2 = (f32[16,256]{1,0:T(8,128)S(1)}, f32[16,256]{1,0:T(8,128)}, u32[]{:S(2)}) copy-start(f32[16,256]{1,0:T(8,128)} %constant.54.clone) | copy-start | bytes 49156
  127.3 184.0 %copy-start.1 = (f32[16,256]{1,0:T(8,128)S(1)}, f32[16,256]{1,0:T(8,128)}, u32[]{:S(2)}) copy-start(f32[16,256]{1,0:T(8,128)} %constant.55.clone) | copy-start | bytes 49156
  372.8 8.0 %copy-start.3 = (s32[4096]{0:T(1024)S(1)}, s32[4096]{0:T(1024)}, u32[]{:S(2)}) copy-start(s32[4096]{0:T(1024)} %param.21) | copy-start | bytes 49156
  372.8 8.0 %copy-start.5 = (f32[64]{0:T(128)S(1)}, f32[64]{0:T(128)}, u32[]{:S(2)}) copy-start(f32[64]{0:T(128)} %param.20) | copy-start | bytes 772
  372.8 192.7 %all-to-all-start.2 = ((f32[32,2,128,256]{3,2,1,0:T(8,128)}), f32[32,2,128,256]{3,2,1,0:T(8,128)}, u32[]{:S(2)}, u32[]{:S(2)}) async-start(f32[32,2,128,256]{3,2,1,0:T(8,128)} %time_stage.1), calls=%async_computation.2 | async-start | bytes 16777216 | tf_op jit(solution)/shard_map/all_to_all | solution.py:392

commit v2 on v1

--- a/solution.py
+++ b/solution.py
@@ -256,6 +256,231 @@
         compiler_params=params(),
         name="channel_inverse",
     )(x, *tables)
+
+
+def others(devices, visit):
+    spread = math.gcd(4, devices)
+
+    @pl.loop(1, devices)
+    def _(i):
+        visit(lax.rem(i, spread) * (devices // spread) + i // spread)
+
+
+def greet(devices, owners, me):
+    barrier = pltpu.get_barrier_semaphore()
+
+    def hail(step):
+        to = lax.rem(me + step, devices)
+        pl.semaphore_signal(
+            barrier, inc=1, device_id=(to // owners, lax.rem(to, owners)),
+            device_id_type=pl.DeviceIdType.MESH,
+        )
+
+    others(devices, hail)
+    pl.semaphore_wait(barrier, devices - 1)
+
+
+def send_out_kernel(
+    x_ref, table_ref, first_ref, cos_ref, sin_ref, out_ref,
+    got, held, ready, own_in, own_out, chan_send, chan_recv, full_send, full_recv,
+):
+    owners, rows, _ = x_ref.shape
+    chunks, devices, _, block, _ = ready.shape
+    line, place = lax.axis_index("tm"), lax.axis_index("chan")
+    me = line * owners + place
+
+    def part(q):
+        return pl.ds(pl.multiple_of(q * block, block), block)
+
+    def across(q, step, back=False):
+        to = lax.rem(place + step, owners)
+        source = lax.rem(place + owners - step, owners) if back else place
+        return pltpu.make_async_remote_copy(
+            src_ref=x_ref.at[to, part(q)], dst_ref=got.at[source, part(q)],
+            send_sem=chan_send.at[q, step], recv_sem=chan_recv.at[q, step],
+            device_id=(line, to), device_id_type=pl.DeviceIdType.MESH,
+        )
+
+    def everywhere(q, step, back=False):
+        to = lax.rem(me + step, devices)
+        source = lax.rem(me + devices - step, devices) if back else me
+        return pltpu.make_async_remote_copy(
+            src_ref=ready.at[q, to], dst_ref=out_ref.at[source, :, part(q)],
+            send_sem=full_send.at[q, step], recv_sem=full_recv.at[q, step],
+            device_id=(to // owners, lax.rem(to, owners)), device_id_type=pl.DeviceIdType.MESH,
+        )
+
+    def take_own(q):
+        return pltpu.make_async_copy(x_ref.at[place, part(q)], got.at[place, part(q)], own_in.at[q])
+
+    def give_own(q):
+        return pltpu.make_async_copy(ready.at[q, me], out_ref.at[me, :, part(q)], own_out.at[q])
+
+    def begin(q):
+        take_own(q).start()
+        for step in range(1, owners):
+            across(q, step).start()
+
+    greet(devices, owners, me)
+    ahead = min(2, chunks)
+    for q in range(ahead):
+        begin(q)
+
+    @pl.loop(0, chunks)
+    def _(q):
+        take_own(q).wait()
+        for step in range(1, owners):
+            across(q, step, True).wait_recv()
+
+        @pl.when(q + ahead < chunks)
+        def _():
+            begin(q + ahead)
+
+        forward_kernel(
+            got.at[:, part(q)], table_ref, first_ref, cos_ref, sin_ref, ready.at[q], held
+        )
+        give_own(q).start()
+        others(devices, lambda step: everywhere(q, step).start())
+
+    @pl.loop(0, chunks)
+    def _(q):
+        for step in range(1, owners):
+            across(q, step).wait_send()
+        give_own(q).wait()
+
+        def finish(step):
+            everywhere(q, step).wait_send()
+            everywhere(q, step, True).wait_recv()
+
+        others(devices, finish)
+
+
+def send_back_kernel(
+    x_ref, table_ref, first_ref, cos_ref, sin_ref, gain_ref, out_ref,
+    got, held, ready, own_in, own_out, chan_send, chan_recv, full_send, full_recv,
+):
+    owners, rows, _ = out_ref.shape
+    devices = x_ref.shape[0]
+    chunks = own_in.shape[0]
+    block = rows // chunks
+    line, place = lax.axis_index("tm"), lax.axis_index("chan")
+    me = line * owners + place
+
+    def part(q):
+        return pl.ds(pl.multiple_of(q * block, block), block)
+
+    def across(q, step, back=False):
+        to = lax.rem(place + step, owners)
+        source = lax.rem(place + owners - step, owners) if back else place
+        return pltpu.make_async_remote_copy(
+            src_ref=ready.at[to, part(q)], dst_ref=out_ref.at[source, part(q)],
+            send_sem=chan_send.at[q, step], recv_sem=chan_recv.at[q, step],
+            device_id=(line, to), device_id_type=pl.DeviceIdType.MESH,
+        )
+
+    def everywhere(q, step, back=False):
+        to = lax.rem(me + step, devices)
+        source = lax.rem(me + devices - step, devices) if back else me
+        return pltpu.make_async_remote_copy(
+            src_ref=x_ref.at[to, :, part(q)], dst_ref=got.at[source, :, part(q)],
+            send_sem=full_send.at[q, step], recv_sem=full_recv.at[q, step],
+            device_id=(to // owners, lax.rem(to, owners)), device_id_type=pl.DeviceIdType.MESH,
+        )
+
+    def take_own(q):
+        return pltpu.make_async_copy(x_ref.at[me, :, part(q)], got.at[me, :, part(q)], own_in.at[q])
+
+    def give_own(q):
+        return pltpu.make_async_copy(ready.at[place, part(q)], out_ref.at[place, part(q)], own_out.at[q])
+
+    def begin(q):
+        take_own(q).start()
+        others(devices, lambda step: everywhere(q, step).start())
+
+    greet(devices, owners, me)
+    ahead = min(2, chunks)
+    for q in range(ahead):
+        begin(q)
+
+    @pl.loop(0, chunks)
+    def _(q):
+        take_own(q).wait()
+        others(devices, lambda step: everywhere(q, step, True).wait_recv())
+
+        @pl.when(q + ahead < chunks)
+        def _():
+            begin(q + ahead)
+
+        inverse_kernel(
+            got.at[:, :, part(q)], table_ref, first_ref, cos_ref, sin_ref, gain_ref,
+            ready.at[:, part(q)], held,
+        )
+        give_own(q).start()
+        for step in range(1, owners):
+            across(q, step).start()
+
+    @pl.loop(0, chunks)
+    def _(q):
+        others(devices, lambda step: everywhere(q, step).wait_send())
+        give_own(q).wait()
+        for step in range(1, owners):
+            across(q, step).wait_send()
+            across(q, step, True).wait_recv()
+
+
+CHUNK = 32
+
+
+def exchange_semaphores(chunks, owners, devices):
+    dma = pltpu.SemaphoreType.DMA
+    return [
+        dma((chunks,)), dma((chunks,)), dma((chunks, owners)), dma((chunks, owners)),
+        dma((chunks, devices)), dma((chunks, devices)),
+    ]
+
+
+def exchange_call(kernel, ident, operands, out_shape, buffers, sizes):
+    anywhere = pl.BlockSpec(memory_space=pl.ANY)
+    inside = pl.BlockSpec(memory_space=pltpu.VMEM)
+    return pl.pallas_call(
+        kernel,
+        in_specs=[anywhere] + [inside] * (len(operands) - 1),
+        out_specs=anywhere,
+        out_shape=jax.ShapeDtypeStruct(out_shape, F32),
+        scratch_shapes=[pltpu.VMEM(b, F32) for b in buffers] + exchange_semaphores(*sizes),
+        compiler_params=pltpu.CompilerParams(
+            vmem_limit_bytes=56 * 2**20, collective_id=ident, has_side_effects=True
+        ),
+        name=kernel.__name__,
+    )(*operands)
+
+
+def send_out(x, devices):
+    owners, rows, width = x.shape
+    channels = owners * width
+    slots = channels // WIDE // 2
+    chunks = rows // min(CHUNK, rows)
+    block = rows // chunks
+    table, first, cos, sin = channel_tables(channels)
+    operands = [x] + [jnp.asarray(t) for t in (halves(table), halves(first), cos, sin)]
+    buffers = [(owners, rows, width), (slots, block, 2 * WIDE), (chunks, slots, 2, block, WIDE)]
+    return exchange_call(
+        send_out_kernel, 0, operands, (devices, 2, rows, WIDE), buffers, (chunks, owners, devices)
+    )
+
+
+def send_back(x, gains, owners):
+    slots, _, rows, _ = x.shape
+    channels = 2 * slots * WIDE
+    width = channels // owners
+    chunks = rows // min(CHUNK, rows)
+    block = rows // chunks
+    table, first, cos, sin = channel_tables(channels)
+    operands = [x] + [jnp.asarray(t) for t in (halves(table.T), halves(first.T), cos, sin)] + [gains]
+    buffers = [x.shape, (slots, block, 2 * WIDE), (owners, rows, width)]
+    return exchange_call(
+        send_back_kernel, 1, operands, (owners, rows, width), buffers, (chunks, owners, slots)
+    )
 
 
 def time_kernel(x_ref, table_ref, cos_ref, sin_ref, factor_ref, fir_ref, out_ref, held, line):
@@ -405,6 +630,11 @@
     gains = lax.all_gather(gains, "chan")
     factor = mask_factor(band_edges, channels, piece, padded)
 
+    if devices == slots:
+        spectra = send_out(traces.reshape(owners, length // owners, width), devices)
+        spectra = time_stage(spectra, factor, taps)
+        return send_back(spectra, gains, owners).reshape(length, width)
+
     gathered = exchange(traces.reshape(owners, length // owners, width), "chan")
     spectra = exchange(regroup(channel_forward(gathered), devices), AXES)
     if padded > piece:

time: 687 us -> 518 us (0.75)
  Pallas kernels: 96.2 us -> 491 us
  waiting for transfers between devices: 314 us -> 0 us
  blocking collectives: 245 us -> 6.36 us
  starting transfers between devices: 14.5 us -> 0 us
    pallas_call x2, Pallas kernels: 36.6 us -> 432 us  [exchange_call(): pl.pallas_call(kernel, in_specs=[anywhere] + [inside] * (len(operands) -...]
    all_to_all x2 -> x0, waiting for transfers between devices: 314 us -> none  [exchange(): return lax.all_to_all(x, axes, split_axis=0, concat_axis=0, tiled=True)]
    all_to_all x2 -> x0, blocking collectives: 197 us -> none  [exchange(): return lax.all_to_all(x, axes, split_axis=0, concat_axis=0, tiled=True)]
    all_gather x1, blocking collectives: 47.7 us -> 6.36 us  [per_device(): gains = lax.all_gather(gains, 'chan')]
    all_to_all x2 -> x0, starting transfers between devices: 14.5 us -> none  [exchange(): return lax.all_to_all(x, axes, split_axis=0, concat_axis=0, tiled=True)]
  transfers between devices with their start and end apart: 2 -> 0, of which waited for: 2 -> 0; matrix products, arithmetic and copies ran while one was open for 1% -> 0% of each run, Pallas kernels for 0% -> 0%
where the time goes in v2:
time: 518 us
  Pallas kernels  491 us (95%)
  local copies, waits for them, and re-layouts  14.8 us (3%)
  blocking collectives  6.36 us (1%)
    pallas_call x2, Pallas kernels, exchange_call(): pl.pallas_call(kernel, in_specs=[anywhere] + [inside] * (len(operands) -...  432 us
    pallas_call x1, Pallas kernels, time_stage(): pl.pallas_call(time_kernel, grid=(piece // LANES,), in_specs=[block, whol...  59.7 us

profile of v2, /device:TPU:1, one launch (start us, length us, event | category | flops | bytes accessed | tf_op | source)
XLA Modules:
  0.0 517.6 jit_solution(15225856238532598957)
XLA Ops:
  0.0 0.0 copy-start.3
  0.0 0.8 compare_select_fusion
  0.8 0.8 dynamic_slice.3
  1.5 0.9 reshape.51
  2.5 0.1 copy.23
  2.5 0.1 copy.24
  2.6 3.0 select_multiply_fusion.factor_ref
  5.6 0.0 copy-done.3
  5.6 0.1 pad.4
  5.7 0.5 tile.10
  6.3 0.1 reshape.52
  6.4 0.1 reduce-precision_convert_fusion
  6.5 0.8 pad_maximum_fusion.fir_ref
  7.3 0.0 copy-start.1
  7.3 0.0 copy-start
  7.3 208.8 %send_out_kernel.1.x_ref = f32[32,2,128,256]{3,2,1,0:T(8,128)} custom-call(f32[4,128,4096]{2,1,0:T(8,128)} %bitcast.8, bf16[2,512,512]{2,1,0:T(8,128)(2,1)} %constant.49.clone.table_ref, bf16[2,512,512]{2,1,0:T(8,128)(2,1)} %constant.50.clone.first_ref, f32[32,256]{1,0:T(8,128)} %constant.51.clone.cos_ref, f32[32,256]{1,0:T(8,128)} %constant.52.clone.sin_ref), custom_call_target="tpu_custom_call" | custom-call | tf_op jit(solution)/shard_map/send_out_kernel/pallas_call | solution.py:445
  216.1 0.0 copy-done.1
  216.1 1.9 broadcast_in_dim.49.cos_ref
  218.1 0.0 copy-done
  218.1 1.9 broadcast_in_dim.50.sin_ref
  220.0 0.0 copy-start.2
  220.0 0.0 copy-start.4
  220.0 59.7 %time_stage.1.x_ref = f32[32,2,128,256]{3,2,1,0:T(8,128)} custom-call(f32[32,2,128,256]{3,2,1,0:T(8,128)} %send_out_kernel.1.x_ref, bf16[2,512,256]{2,1,0:T(8,128)(2,1)} %constant.53.clone.table_ref, f32[16,256,128]{2,1,0:T(8,128)} %broadcast_in_dim.49.cos_ref, f32[16,256,128]{2,1,0:T(8,128)} %broadcast_in_dim.50.sin_ref, ...), custom_call_target="tpu_custom_call" | custom-call | tf_op jit(solution)/shard_map/time_stage/pallas_call | solution.py:564
  279.7 0.0 copy-done.2
  279.7 0.0 copy-done.4
  279.7 0.2 select_reduce_fusion
  279.9 6.4 %all-gather = f32[16384]{0:T(1024)S(1)} all-gather(f32[4096]{0:T(1024)S(1)} %select_reduce_fusion), channel_id=2, replica_groups=mesh['tm'=8,'chan'=4] {'chan'}, dimensions={0}, use_global_device_ids=true | all-gather | bytes 81920 | tf_op jit(solution)/shard_map/all_gather | solution.py:630
  286.3 0.7 reshape.54.gain_ref
  287.0 222.9 %send_back_kernel.1 = f32[4,128,4096]{2,1,0:T(8,128)} custom-call(f32[32,2,128,256]{3,2,1,0:T(8,128)} %time_stage.1.x_ref, bf16[2,512,512]{2,1,0:T(8,128)(2,1)} %constant.56.clone.table_ref, bf16[2,512,512]{2,1,0:T(8,128)(2,1)} %constant.57.clone.first_ref, f32[32,256]{1,0:T(8,128)} %constant.51.clone.cos_ref, f32[32,256]{1,0:T(8,128)} %constant.52.clone.sin_ref, ...), custom_call_target="tpu_custom_call" | custom-call | tf_op jit(solution)/shard_map/send_back_kernel/pallas_call | solution.py:445
  509.9 7.8 %copy.26 = f32[512,4096]{1,0:T(8,128)} copy(f32[512,4096]{1,0:T(8,128)} %bitcast.7) | data formatting | bytes 16777216
  (3 shorter events, 0.1 us)
Async XLA Ops:
  0.0 5.6 %copy-start.3 = (f32[255]{0:T(256)S(1)}, f32[255]{0:T(256)}, u32[]{:S(2)}) copy-start(f32[255]{0:T(256)} %param.19) | copy-start | bytes 3064
  7.3 208.8 %copy-start.1 = (f32[16,256]{1,0:T(8,128)S(1)}, f32[16,256]{1,0:T(8,128)}, u32[]{:S(2)}) copy-start(f32[16,256]{1,0:T(8,128)} %constant.54.clone) | copy-start | bytes 49156
  7.3 210.8 %copy-start = (f32[16,256]{1,0:T(8,128)S(1)}, f32[16,256]{1,0:T(8,128)}, u32[]{:S(2)}) copy-start(f32[16,256]{1,0:T(8,128)} %constant.55.clone) | copy-start | bytes 49156
  220.0 59.7 %copy-start.2 = (s32[4096]{0:T(1024)S(1)}, s32[4096]{0:T(1024)}, u32[]{:S(2)}) copy-start(s32[4096]{0:T(1024)} %param.21) | copy-start | bytes 49156
  220.0 59.7 %copy-start.4 = (f32[64]{0:T(128)S(1)}, f32[64]{0:T(128)}, u32[]{:S(2)}) copy-start(f32[64]{0:T(128)} %param.20) | copy-start | bytes 772

commit v3 on v2

--- a/solution.py
+++ b/solution.py
@@ -175,7 +175,7 @@
     out_ref[0, 1] = y[:, WIDE:]
 
 
-def inverse_kernel(x_ref, table_ref, first_ref, cos_ref, sin_ref, gain_ref, out_ref, held):
+def inverse_kernel(x_ref, table_ref, first_ref, cos_ref, sin_ref, out_ref, held):
     owners, rows, width = out_ref.shape
     slots = held.shape[0]
     per = width // WIDE
@@ -206,8 +206,7 @@
             for j in range(owners):
                 for b in range(per):
                     place = pl.ds(b * WIDE + lane, LANES)
-                    gain = gain_ref[pl.ds(j, 1), place]
-                    out_ref[j, at, place] = y[j * per + b] * gain
+                    out_ref[j, at, place] = y[j * per + b]
 
 
 def whole(shape):
@@ -238,13 +237,13 @@
     )(x, *tables)
 
 
-def channel_inverse(x, gains, owners):
+def channel_inverse(x, owners):
     slots, _, rows, _ = x.shape
     channels = 2 * slots * WIDE
     width = channels // owners
     block = min(32, rows)
     table, first, cos, sin = channel_tables(channels)
-    tables = [jnp.asarray(halves(table.T)), jnp.asarray(halves(first.T)), jnp.asarray(cos), jnp.asarray(sin), gains]
+    tables = [jnp.asarray(halves(table.T)), jnp.asarray(halves(first.T)), jnp.asarray(cos), jnp.asarray(sin)]
     return pl.pallas_call(
         inverse_kernel,
         grid=(rows // block,),
@@ -356,15 +355,19 @@
 
 
 def send_back_kernel(
-    x_ref, table_ref, first_ref, cos_ref, sin_ref, gain_ref, out_ref,
-    got, held, ready, own_in, own_out, chan_send, chan_recv, full_send, full_recv,
+    x_ref, turn_ref, cos_t_ref, sin_t_ref, factor_ref, fir_ref,
+    table_ref, first_ref, cos_ref, sin_ref, out_ref,
+    lanes, line_held, padded, got, held, ready,
+    own_in, own_half, own_part, own_out, half_send, half_recv,
+    chan_send, chan_recv, full_send, full_recv,
 ):
     owners, rows, _ = out_ref.shape
     devices = x_ref.shape[0]
-    chunks = own_in.shape[0]
+    chunks = own_part.shape[0]
     block = rows // chunks
     line, place = lax.axis_index("tm"), lax.axis_index("chan")
     me = line * owners + place
+    first_half, second_half = pl.ds(0, LANES), pl.ds(LANES, LANES)
 
     def part(q):
         return pl.ds(pl.multiple_of(q * block, block), block)
@@ -378,33 +381,69 @@
             device_id=(line, to), device_id_type=pl.DeviceIdType.MESH,
         )
 
+    def half(step, back=False):
+        to = lax.rem(me + step, devices)
+        source = lax.rem(me + devices - step, devices) if back else me
+        return pltpu.make_async_remote_copy(
+            src_ref=lanes.at[0, to], dst_ref=got.at[source, :, :, first_half],
+            send_sem=half_send.at[step], recv_sem=half_recv.at[step],
+            device_id=(to // owners, lax.rem(to, owners)), device_id_type=pl.DeviceIdType.MESH,
+        )
+
     def everywhere(q, step, back=False):
         to = lax.rem(me + step, devices)
         source = lax.rem(me + devices - step, devices) if back else me
         return pltpu.make_async_remote_copy(
-            src_ref=x_ref.at[to, :, part(q)], dst_ref=got.at[source, :, part(q)],
+            src_ref=lanes.at[1, to, :, part(q)], dst_ref=got.at[source, :, part(q), second_half],
             send_sem=full_send.at[q, step], recv_sem=full_recv.at[q, step],
             device_id=(to // owners, lax.rem(to, owners)), device_id_type=pl.DeviceIdType.MESH,
         )
 
-    def take_own(q):
-        return pltpu.make_async_copy(x_ref.at[me, :, part(q)], got.at[me, :, part(q)], own_in.at[q])
+    def take_own(side):
+        return pltpu.make_async_copy(
+            x_ref.at[:, :, :, pl.ds(side * LANES, LANES)], lanes.at[side], own_in.at[side]
+        )
+
+    def keep_half():
+        return pltpu.make_async_copy(lanes.at[0, me], got.at[me, :, :, first_half], own_half)
+
+    def keep_part(q):
+        return pltpu.make_async_copy(
+            lanes.at[1, me, :, part(q)], got.at[me, :, part(q), second_half], own_part.at[q]
+        )
 
     def give_own(q):
         return pltpu.make_async_copy(ready.at[place, part(q)], out_ref.at[place, part(q)], own_out.at[q])
 
     def begin(q):
-        take_own(q).start()
+        keep_part(q).start()
         others(devices, lambda step: everywhere(q, step).start())
 
+    def transform(side):
+        time_kernel(
+            lanes.at[side], turn_ref, cos_t_ref, sin_t_ref,
+            factor_ref.at[:, :, pl.ds(side * LANES, LANES)], fir_ref, lanes.at[side],
+            line_held, padded,
+        )
+
+    take_own(0).start()
+    take_own(1).start()
     greet(devices, owners, me)
+    take_own(0).wait()
+    transform(0)
+    keep_half().start()
+    others(devices, lambda step: half(step).start())
+    take_own(1).wait()
+    transform(1)
     ahead = min(2, chunks)
     for q in range(ahead):
         begin(q)
+    keep_half().wait()
+    others(devices, lambda step: half(step, True).wait_recv())
 
     @pl.loop(0, chunks)
     def _(q):
-        take_own(q).wait()
+        keep_part(q).wait()
         others(devices, lambda step: everywhere(q, step, True).wait_recv())
 
         @pl.when(q + ahead < chunks)
@@ -412,12 +451,14 @@
             begin(q + ahead)
 
         inverse_kernel(
-            got.at[:, :, part(q)], table_ref, first_ref, cos_ref, sin_ref, gain_ref,
+            got.at[:, :, part(q)], table_ref, first_ref, cos_ref, sin_ref,
             ready.at[:, part(q)], held,
         )
         give_own(q).start()
         for step in range(1, owners):
             across(q, step).start()
+
+    others(devices, lambda step: half(step).wait_send())
 
     @pl.loop(0, chunks)
     def _(q):
@@ -428,7 +469,8 @@
             across(q, step, True).wait_recv()
 
 
-CHUNK = 32
+CHUNK_OUT = 16
+CHUNK_BACK = 32
 
 
 def exchange_semaphores(chunks, owners, devices):
@@ -439,7 +481,7 @@
     ]
 
 
-def exchange_call(kernel, ident, operands, out_shape, buffers, sizes):
+def exchange_call(kernel, ident, operands, out_shape, scratch):
     anywhere = pl.BlockSpec(memory_space=pl.ANY)
     inside = pl.BlockSpec(memory_space=pltpu.VMEM)
     return pl.pallas_call(
@@ -447,7 +489,7 @@
         in_specs=[anywhere] + [inside] * (len(operands) - 1),
         out_specs=anywhere,
         out_shape=jax.ShapeDtypeStruct(out_shape, F32),
-        scratch_shapes=[pltpu.VMEM(b, F32) for b in buffers] + exchange_semaphores(*sizes),
+        scratch_shapes=scratch,
         compiler_params=pltpu.CompilerParams(
             vmem_limit_bytes=56 * 2**20, collective_id=ident, has_side_effects=True
         ),
@@ -459,28 +501,34 @@
     owners, rows, width = x.shape
     channels = owners * width
     slots = channels // WIDE // 2
-    chunks = rows // min(CHUNK, rows)
-    block = rows // chunks
+    block = min(CHUNK_OUT, rows)
+    chunks = rows // block
     table, first, cos, sin = channel_tables(channels)
     operands = [x] + [jnp.asarray(t) for t in (halves(table), halves(first), cos, sin)]
     buffers = [(owners, rows, width), (slots, block, 2 * WIDE), (chunks, slots, 2, block, WIDE)]
-    return exchange_call(
-        send_out_kernel, 0, operands, (devices, 2, rows, WIDE), buffers, (chunks, owners, devices)
-    )
-
-
-def send_back(x, gains, owners):
+    scratch = [pltpu.VMEM(b, F32) for b in buffers] + exchange_semaphores(chunks, owners, devices)
+    return exchange_call(send_out_kernel, 0, operands, (devices, 2, rows, WIDE), scratch)
+
+
+def send_back(x, factor, taps, owners):
     slots, _, rows, _ = x.shape
     channels = 2 * slots * WIDE
     width = channels // owners
-    chunks = rows // min(CHUNK, rows)
-    block = rows // chunks
+    block = min(CHUNK_BACK, rows)
+    chunks = rows // block
     table, first, cos, sin = channel_tables(channels)
-    operands = [x] + [jnp.asarray(t) for t in (halves(table.T), halves(first.T), cos, sin)] + [gains]
-    buffers = [x.shape, (slots, block, 2 * WIDE), (owners, rows, width)]
-    return exchange_call(
-        send_back_kernel, 1, operands, (owners, rows, width), buffers, (chunks, owners, slots)
-    )
+    operands = [x, *time_tables(slots * rows), factor, fir_table(taps)]
+    operands += [jnp.asarray(t) for t in (halves(table.T), halves(first.T), cos, sin)]
+    samples = slots * rows
+    buffers = [
+        (2, slots, 2, rows, LANES), (2, samples // WIDE, WIDE, LANES),
+        (2, samples + 2 * LANES, LANES), x.shape, (slots, block, 2 * WIDE), (owners, rows, width),
+    ]
+    dma = pltpu.SemaphoreType.DMA
+    scratch = [pltpu.VMEM(b, F32) for b in buffers]
+    scratch += [dma((2,)), dma(()), dma((chunks,)), dma((chunks,)), dma((slots,)), dma((slots,))]
+    scratch += exchange_semaphores(chunks, owners, slots)[2:]
+    return exchange_call(send_back_kernel, 1, operands, (owners, rows, width), scratch)
 
 
 def time_kernel(x_ref, table_ref, cos_ref, sin_ref, factor_ref, fir_ref, out_ref, held, line):
@@ -547,18 +595,23 @@
     return jnp.stack([high, table - high]).astype(jnp.bfloat16)
 
 
+def time_tables(samples):
+    radix = samples // WIDE
+    a = np.arange(WIDE)
+    cos, sin = turn(a[:, None] * a[None, :], WIDE)
+    table = jnp.asarray(halves(np.concatenate([cos, sin], axis=0)))
+    spread = (radix, WIDE, LANES)
+    turns = turn(np.arange(radix)[:, None] * a[None, :], samples)
+    return [table] + [
+        jnp.asarray(np.broadcast_to(t.astype(np.float32)[:, :, None], spread)) for t in turns
+    ]
+
+
 def time_stage(x, factor, taps):
     devices, _, rows, piece = x.shape
     samples = devices * rows
     radix = samples // WIDE
-    a = np.arange(WIDE)
-    cos, sin = turn(a[:, None] * a[None, :], WIDE)
-    table = jnp.asarray(halves(np.concatenate([cos, sin], axis=0)))
-    cos_t, sin_t = turn(np.arange(radix)[:, None] * a[None, :], samples)
-    turns = [
-        jnp.broadcast_to(jnp.asarray(t.astype(np.float32))[:, :, None], (radix, WIDE, LANES))
-        for t in (cos_t, sin_t)
-    ]
+    table, *turns = time_tables(samples)
     fir = fir_table(taps)
     block = pl.BlockSpec((devices, 2, rows, LANES), lambda i: (0, 0, 0, i))
     return pl.pallas_call(
@@ -627,13 +680,12 @@
     padded = max(piece, LANES)
     matches = gain_index[:, None] == jnp.arange(gain_table.shape[0], dtype=jnp.int32)[None, :]
     gains = jnp.sum(jnp.where(matches, gain_table[None, :], 0.0), axis=1)
-    gains = lax.all_gather(gains, "chan")
     factor = mask_factor(band_edges, channels, piece, padded)
 
     if devices == slots:
         spectra = send_out(traces.reshape(owners, length // owners, width), devices)
-        spectra = time_stage(spectra, factor, taps)
-        return send_back(spectra, gains, owners).reshape(length, width)
+        local = send_back(spectra, factor, taps, owners)
+        return local.reshape(length, width) * gains[None, :]
 
     gathered = exchange(traces.reshape(owners, length // owners, width), "chan")
     spectra = exchange(regroup(channel_forward(gathered), devices), AXES)
@@ -643,8 +695,8 @@
     if padded > piece:
         spectra = spectra[..., :piece]
     returned = ungroup(exchange(spectra, AXES), slots)
-    local = exchange(channel_inverse(returned, gains, owners), "chan")
-    return local.reshape(length, width)
+    local = exchange(channel_inverse(returned, owners), "chan")
+    return local.reshape(length, width) * gains[None, :]
 
 
 def solution(mesh):

time: 518 us -> 506 us (0.977)
  local copies, waits for them, and re-layouts: 14.8 us -> 6.39 us
  other arithmetic: 4.96 us -> 13 us
  blocking collectives: 6.36 us -> 0 us
    pallas_call x1 -> x0, Pallas kernels: 59.7 us -> none  [time_stage(): pl.pallas_call(time_kernel, grid=(piece // LANES,), in_specs=[block, whol...]
    pallas_call x2, Pallas kernels: 432 us -> 486 us  [exchange_call(): pl.pallas_call(kernel, in_specs=[anywhere] + [inside] * (len(operands) -...]
    mul x0 -> x1, other arithmetic: none -> 8.1 us  [per_device(): return local.reshape(length, width) * gains[None, :]]
    unnamed x11 -> x10, local copies, waits for them, and re-layouts: 7.79 us -> 0.02 us
    all_gather x1 -> x0, blocking collectives: 6.36 us -> none  [per_device(): gains = lax.all_gather(gains, 'chan')]
where the time goes in v3:
time: 506 us
  Pallas kernels  486 us (96%)
  other arithmetic  13 us (3%)
  local copies, waits for them, and re-layouts  6.39 us (1%)
    pallas_call x2, Pallas kernels, exchange_call(): pl.pallas_call(kernel, in_specs=[anywhere] + [inside] * (len(operands) -...  486 us

profile of v3, /device:TPU:1, one launch (start us, length us, event | category | flops | bytes accessed | tf_op | source)
XLA Modules:
  0.0 505.7 jit_solution(10934629451605540913)
XLA Ops:
  0.0 0.0 copy-start.3
  0.0 0.8 compare_select_fusion
  0.8 0.8 dynamic_slice.3
  1.5 0.9 reshape.50
  2.5 0.1 copy.21
  2.5 0.1 copy.22
  2.6 3.0 select_multiply_fusion.factor_ref
  5.6 0.0 copy-done.3
  5.6 0.1 pad.4
  5.7 0.5 tile.10
  6.3 0.1 reshape.51
  6.3 0.1 reduce-precision_convert_fusion
  6.4 0.9 pad_maximum_fusion.fir_ref
  7.3 0.0 copy-start.1
  7.3 0.0 copy-start
  7.3 205.2 %send_out_kernel.1.x_ref = f32[32,2,128,256]{3,2,1,0:T(8,128)} custom-call(f32[4,128,4096]{2,1,0:T(8,128)} %bitcast.8, bf16[2,512,512]{2,1,0:T(8,128)(2,1)} %constant.49.clone.table_ref, bf16[2,512,512]{2,1,0:T(8,128)(2,1)} %constant.50.clone.first_ref, f32[32,256]{1,0:T(8,128)} %constant.51.clone.cos_ref, f32[32,256]{1,0:T(8,128)} %constant.52.clone.sin_ref), custom_call_target="tpu_custom_call" | custom-call | tf_op jit(solution)/shard_map/send_out_kernel/pallas_call | solution.py:487
  212.4 0.0 copy-done.1
  212.5 1.9 jit_solution_.6.cos_t_ref
  214.4 0.0 copy-done
  214.4 1.9 jit_solution_.7.sin_t_ref
  216.3 0.0 copy-start.2
  216.3 0.0 copy-start.4
  216.3 281.1 %send_back_kernel.1 = f32[4,128,4096]{2,1,0:T(8,128)} custom-call(f32[32,2,128,256]{3,2,1,0:T(8,128)} %send_out_kernel.1.x_ref, bf16[2,512,256]{2,1,0:T(8,128)(2,1)} %constant.53.clone.turn_ref, f32[16,256,128]{2,1,0:T(8,128)} %jit_solution_.6.cos_t_ref, f32[16,256,128]{2,1,0:T(8,128)} %jit_solution_.7.sin_t_ref, ...), custom_call_target="tpu_custom_call" | custom-call | tf_op jit(solution)/shard_map/send_back_kernel/pallas_call | solution.py:487
  497.4 0.0 copy-done.2
  497.4 0.0 copy-done.4
  497.4 0.2 select_reduce_fusion
  497.6 8.1 %bitcast_multiply_fusion = f32[512,4096]{1,0:T(8,128)} fusion(f32[4,128,4096]{2,1,0:T(8,128)} %send_back_kernel.1, f32[4096]{0:T(1024)S(1)} %select_reduce_fusion), kind=kLoop, calls=%fused_computation | loop fusion | flops 2097152 | bytes 16793600 | tf_op jit(solution)/shard_map/mul | solution.py:688
  (3 shorter events, 0.1 us)
Async XLA Ops:
  0.0 5.6 %copy-start.3 = (f32[255]{0:T(256)S(1)}, f32[255]{0:T(256)}, u32[]{:S(2)}) copy-start(f32[255]{0:T(256)} %param.19) | copy-start | bytes 3064
  7.3 205.2 %copy-start.1 = (f32[16,256]{1,0:T(8,128)S(1)}, f32[16,256]{1,0:T(8,128)}, u32[]{:S(2)}) copy-start(f32[16,256]{1,0:T(8,128)} %constant.54.clone) | copy-start | bytes 49156
  7.3 207.1 %copy-start = (f32[16,256]{1,0:T(8,128)S(1)}, f32[16,256]{1,0:T(8,128)}, u32[]{:S(2)}) copy-start(f32[16,256]{1,0:T(8,128)} %constant.55.clone) | copy-start | bytes 49156
  216.3 281.1 %copy-start.2 = (s32[4096]{0:T(1024)S(1)}, s32[4096]{0:T(1024)}, u32[]{:S(2)}) copy-start(s32[4096]{0:T(1024)} %param.21) | copy-start | bytes 49156
  216.3 281.1 %copy-start.4 = (f32[64]{0:T(128)S(1)}, f32[64]{0:T(128)}, u32[]{:S(2)}) copy-start(f32[64]{0:T(128)} %param.20) | copy-start | bytes 772

commit v4 on v3

--- a/solution.py
+++ b/solution.py
@@ -175,7 +175,11 @@
     out_ref[0, 1] = y[:, WIDE:]
 
 
-def inverse_kernel(x_ref, table_ref, first_ref, cos_ref, sin_ref, out_ref, held):
+def inverse_kernel(x_ref, *refs):
+    inverse_body(lambda at: jnp.concatenate([x_ref[at, 0], x_ref[at, 1]], axis=-1), *refs)
+
+
+def inverse_body(load, table_ref, first_ref, cos_ref, sin_ref, out_ref, held):
     owners, rows, width = out_ref.shape
     slots = held.shape[0]
     per = width // WIDE
@@ -184,11 +188,10 @@
     @pl.loop(0, slots // group)
     def _(step):
         at = pl.ds(step * group, group)
-        x = jnp.concatenate([x_ref[at, 0], x_ref[at, 1]], axis=-1)
-        y = dot_right(x.reshape(group * rows, 2 * WIDE), table_ref)
+        y = dot_right(load(at).reshape(group * rows, 2 * WIDE), table_ref)
         held[at] = y.reshape(group, rows, 2 * WIDE)
 
-    held[0] = dot_right(jnp.concatenate([x_ref[0, 0], x_ref[0, 1]], axis=-1), first_ref)
+    held[0] = dot_right(load(0), first_ref)
 
     @pl.loop(0, rows // 8)
     def _(tile):
@@ -304,7 +307,7 @@
         to = lax.rem(me + step, devices)
         source = lax.rem(me + devices - step, devices) if back else me
         return pltpu.make_async_remote_copy(
-            src_ref=ready.at[q, to], dst_ref=out_ref.at[source, :, part(q)],
+            src_ref=ready.at[q, to], dst_ref=out_ref.at[source * chunks + q],
             send_sem=full_send.at[q, step], recv_sem=full_recv.at[q, step],
             device_id=(to // owners, lax.rem(to, owners)), device_id_type=pl.DeviceIdType.MESH,
         )
@@ -313,7 +316,7 @@
         return pltpu.make_async_copy(x_ref.at[place, part(q)], got.at[place, part(q)], own_in.at[q])
 
     def give_own(q):
-        return pltpu.make_async_copy(ready.at[q, me], out_ref.at[me, :, part(q)], own_out.at[q])
+        return pltpu.make_async_copy(ready.at[q, me], out_ref.at[me * chunks + q], own_out.at[q])
 
     def begin(q):
         take_own(q).start()
@@ -362,12 +365,13 @@
     chan_send, chan_recv, full_send, full_recv,
 ):
     owners, rows, _ = out_ref.shape
-    devices = x_ref.shape[0]
-    chunks = own_part.shape[0]
+    _, devices, chunks, _, _, _ = got.shape
     block = rows // chunks
     line, place = lax.axis_index("tm"), lax.axis_index("chan")
     me = line * owners + place
-    first_half, second_half = pl.ds(0, LANES), pl.ds(LANES, LANES)
+
+    def run(device):
+        return pl.ds(device * chunks, chunks)
 
     def part(q):
         return pl.ds(pl.multiple_of(q * block, block), block)
@@ -385,7 +389,7 @@
         to = lax.rem(me + step, devices)
         source = lax.rem(me + devices - step, devices) if back else me
         return pltpu.make_async_remote_copy(
-            src_ref=lanes.at[0, to], dst_ref=got.at[source, :, :, first_half],
+            src_ref=lanes.at[0, run(to)], dst_ref=got.at[0, source],
             send_sem=half_send.at[step], recv_sem=half_recv.at[step],
             device_id=(to // owners, lax.rem(to, owners)), device_id_type=pl.DeviceIdType.MESH,
         )
@@ -394,7 +398,7 @@
         to = lax.rem(me + step, devices)
         source = lax.rem(me + devices - step, devices) if back else me
         return pltpu.make_async_remote_copy(
-            src_ref=lanes.at[1, to, :, part(q)], dst_ref=got.at[source, :, part(q), second_half],
+            src_ref=lanes.at[1, to * chunks + q], dst_ref=got.at[1, source, q],
             send_sem=full_send.at[q, step], recv_sem=full_recv.at[q, step],
             device_id=(to // owners, lax.rem(to, owners)), device_id_type=pl.DeviceIdType.MESH,
         )
@@ -405,11 +409,11 @@
         )
 
     def keep_half():
-        return pltpu.make_async_copy(lanes.at[0, me], got.at[me, :, :, first_half], own_half)
+        return pltpu.make_async_copy(lanes.at[0, run(me)], got.at[0, me], own_half)
 
     def keep_part(q):
         return pltpu.make_async_copy(
-            lanes.at[1, me, :, part(q)], got.at[me, :, part(q), second_half], own_part.at[q]
+            lanes.at[1, me * chunks + q], got.at[1, me, q], own_part.at[q]
         )
 
     def give_own(q):
@@ -450,8 +454,11 @@
         def _():
             begin(q + ahead)
 
-        inverse_kernel(
-            got.at[:, :, part(q)], table_ref, first_ref, cos_ref, sin_ref,
+        def load(at):
+            return jnp.concatenate([got[side, at, q, p] for p in range(2) for side in range(2)], axis=-1)
+
+        inverse_body(
+            load, table_ref, first_ref, cos_ref, sin_ref,
             ready.at[:, part(q)], held,
         )
         give_own(q).start()
@@ -469,8 +476,7 @@
             across(q, step, True).wait_recv()
 
 
-CHUNK_OUT = 16
-CHUNK_BACK = 32
+CHUNK = 16
 
 
 def exchange_semaphores(chunks, owners, devices):
@@ -501,34 +507,35 @@
     owners, rows, width = x.shape
     channels = owners * width
     slots = channels // WIDE // 2
-    block = min(CHUNK_OUT, rows)
+    block = min(CHUNK, rows)
     chunks = rows // block
     table, first, cos, sin = channel_tables(channels)
     operands = [x] + [jnp.asarray(t) for t in (halves(table), halves(first), cos, sin)]
     buffers = [(owners, rows, width), (slots, block, 2 * WIDE), (chunks, slots, 2, block, WIDE)]
     scratch = [pltpu.VMEM(b, F32) for b in buffers] + exchange_semaphores(chunks, owners, devices)
-    return exchange_call(send_out_kernel, 0, operands, (devices, 2, rows, WIDE), scratch)
-
-
-def send_back(x, factor, taps, owners):
-    slots, _, rows, _ = x.shape
-    channels = 2 * slots * WIDE
-    width = channels // owners
-    block = min(CHUNK_BACK, rows)
-    chunks = rows // block
+    return exchange_call(send_out_kernel, 0, operands, (devices * chunks, 2, block, WIDE), scratch)
+
+
+def send_back(x, factor, taps, owners, devices, channels):
+    pieces, _, block, _ = x.shape
+    samples = pieces * block
+    slots = channels // WIDE // 2
+    chunks = pieces // devices
+    rows = chunks * block
     table, first, cos, sin = channel_tables(channels)
-    operands = [x, *time_tables(slots * rows), factor, fir_table(taps)]
+    operands = [x, *time_tables(samples), factor, fir_table(taps)]
     operands += [jnp.asarray(t) for t in (halves(table.T), halves(first.T), cos, sin)]
-    samples = slots * rows
+    shape = (owners, rows, channels // owners)
     buffers = [
-        (2, slots, 2, rows, LANES), (2, samples // WIDE, WIDE, LANES),
-        (2, samples + 2 * LANES, LANES), x.shape, (slots, block, 2 * WIDE), (owners, rows, width),
+        (2, pieces, 2, block, LANES), (2, samples // WIDE, WIDE, LANES),
+        (2, samples + 2 * LANES, LANES), (2, devices, chunks, 2, block, LANES),
+        (slots, block, 2 * WIDE), shape,
     ]
     dma = pltpu.SemaphoreType.DMA
     scratch = [pltpu.VMEM(b, F32) for b in buffers]
-    scratch += [dma((2,)), dma(()), dma((chunks,)), dma((chunks,)), dma((slots,)), dma((slots,))]
-    scratch += exchange_semaphores(chunks, owners, slots)[2:]
-    return exchange_call(send_back_kernel, 1, operands, (owners, rows, width), scratch)
+    scratch += [dma((2,)), dma(()), dma((chunks,)), dma((chunks,)), dma((devices,)), dma((devices,))]
+    scratch += exchange_semaphores(chunks, owners, devices)[2:]
+    return exchange_call(send_back_kernel, 1, operands, shape, scratch)
 
 
 def time_kernel(x_ref, table_ref, cos_ref, sin_ref, factor_ref, fir_ref, out_ref, held, line):
@@ -536,18 +543,18 @@
     radix = held.shape[1]
     per = WIDE // rows
 
-    for part in range(per):
-        @pl.loop(0, rows // 8)
-        def _(tile):
-            at = pl.ds(pl.multiple_of(tile * 8, 8), 8)
-            to = pl.ds(pl.multiple_of(part * rows + tile * 8, 8), 8)
-            x = [(x_ref[b * per + part, 0, at], x_ref[b * per + part, 1, at]) for b in range(radix)]
-            y = complex_short(x, -1.0)
-            for g in range(radix):
-                re, im = y[g]
-                c, s = cos_ref[g, to], sin_ref[g, to]
-                held[0, g, to] = re * c + im * s
-                held[1, g, to] = im * c - re * s
+    @pl.loop(0, WIDE // 8)
+    def _(tile):
+        part = tile // (rows // 8)
+        at = pl.ds(pl.multiple_of(lax.rem(tile, rows // 8) * 8, 8), 8)
+        to = pl.ds(pl.multiple_of(tile * 8, 8), 8)
+        x = [(x_ref[b * per + part, 0, at], x_ref[b * per + part, 1, at]) for b in range(radix)]
+        y = complex_short(x, -1.0)
+        for g in range(radix):
+            re, im = y[g]
+            c, s = cos_ref[g, to], sin_ref[g, to]
+            held[0, g, to] = re * c + im * s
+            held[1, g, to] = im * c - re * s
 
     @pl.loop(0, radix)
     def _(g):
@@ -684,7 +691,7 @@
 
     if devices == slots:
         spectra = send_out(traces.reshape(owners, length // owners, width), devices)
-        local = send_back(spectra, factor, taps, owners)
+        local = send_back(spectra, factor, taps, owners, devices, channels)
         return local.reshape(length, width) * gains[None, :]
 
     gathered = exchange(traces.reshape(owners, length // owners, width), "chan")

time: 506 us -> 502 us (level)
  no operation moved by 1% of the time
where the time goes in v4:
time: 502 us
  Pallas kernels  482 us (96%)
  other arithmetic  13 us (3%)
  local copies, waits for them, and re-layouts  6.39 us (1%)
    pallas_call x2, Pallas kernels, exchange_call(): pl.pallas_call(kernel, in_specs=[anywhere] + [inside] * (len(operands) -...  482 us

profile of v4, /device:TPU:1, one launch (start us, length us, event | category | flops | bytes accessed | tf_op | source)
XLA Modules:
  0.0 501.9 jit_solution(14986867666674319190)
XLA Ops:
  0.0 0.0 copy-start.3
  0.0 0.8 compare_select_fusion
  0.8 0.8 dynamic_slice.3
  1.5 0.9 reshape.50
  2.5 0.1 copy.21
  2.5 0.1 copy.22
  2.6 3.0 select_multiply_fusion.factor_ref
  5.6 0.0 copy-done.3
  5.6 0.1 pad.4
  5.7 0.5 tile.10
  6.3 0.1 reshape.51
  6.3 0.1 reduce-precision_convert_fusion
  6.4 0.9 pad_maximum_fusion.fir_ref
  7.3 0.0 copy-start.1
  7.3 0.0 copy-start
  7.3 205.2 %send_out_kernel.1.x_ref = f32[256,2,16,256]{3,2,1,0:T(8,128)} custom-call(f32[4,128,4096]{2,1,0:T(8,128)} %bitcast.8, bf16[2,512,512]{2,1,0:T(8,128)(2,1)} %constant.49.clone.table_ref, bf16[2,512,512]{2,1,0:T(8,128)(2,1)} %constant.50.clone.first_ref, f32[32,256]{1,0:T(8,128)} %constant.51.clone.cos_ref, f32[32,256]{1,0:T(8,128)} %constant.52.clone.sin_ref), custom_call_target="tpu_custom_call" | custom-call | tf_op jit(solution)/shard_map/send_out_kernel/pallas_call | solution.py:493
  212.4 0.0 copy-done.1
  212.5 1.9 jit_solution_.6.cos_t_ref
  214.4 0.0 copy-done
  214.4 1.9 jit_solution_.7.sin_t_ref
  216.3 0.0 copy-start.2
  216.3 0.0 copy-start.4
  216.3 277.2 %send_back_kernel.1 = f32[4,128,4096]{2,1,0:T(8,128)} custom-call(f32[256,2,16,256]{3,2,1,0:T(8,128)} %send_out_kernel.1.x_ref, bf16[2,512,256]{2,1,0:T(8,128)(2,1)} %constant.53.clone.turn_ref, f32[16,256,128]{2,1,0:T(8,128)} %jit_solution_.6.cos_t_ref, f32[16,256,128]{2,1,0:T(8,128)} %jit_solution_.7.sin_t_ref, ...), custom_call_target="tpu_custom_call" | custom-call | tf_op jit(solution)/shard_map/send_back_kernel/pallas_call | solution.py:493
  493.5 0.0 copy-done.2
  493.6 0.0 copy-done.4
  493.6 0.2 select_reduce_fusion
  493.8 8.1 %bitcast_multiply_fusion = f32[512,4096]{1,0:T(8,128)} fusion(f32[4,128,4096]{2,1,0:T(8,128)} %send_back_kernel.1, f32[4096]{0:T(1024)S(1)} %select_reduce_fusion), kind=kLoop, calls=%fused_computation | loop fusion | flops 2097152 | bytes 16793600 | tf_op jit(solution)/shard_map/mul | solution.py:695
  (3 shorter events, 0.1 us)
Async XLA Ops:
  0.0 5.6 %copy-start.3 = (f32[255]{0:T(256)S(1)}, f32[255]{0:T(256)}, u32[]{:S(2)}) copy-start(f32[255]{0:T(256)} %param.19) | copy-start | bytes 3064
  7.3 205.2 %copy-start.1 = (f32[16,256]{1,0:T(8,128)S(1)}, f32[16,256]{1,0:T(8,128)}, u32[]{:S(2)}) copy-start(f32[16,256]{1,0:T(8,128)} %constant.54.clone) | copy-start | bytes 49156
  7.3 207.1 %copy-start = (f32[16,256]{1,0:T(8,128)S(1)}, f32[16,256]{1,0:T(8,128)}, u32[]{:S(2)}) copy-start(f32[16,256]{1,0:T(8,128)} %constant.55.clone) | copy-start | bytes 49156
  216.3 277.3 %copy-start.2 = (s32[4096]{0:T(1024)S(1)}, s32[4096]{0:T(1024)}, u32[]{:S(2)}) copy-start(s32[4096]{0:T(1024)} %param.21) | copy-start | bytes 49156
  216.3 277.3 %copy-start.4 = (f32[64]{0:T(128)S(1)}, f32[64]{0:T(128)}, u32[]{:S(2)}) copy-start(f32[64]{0:T(128)} %param.20) | copy-start | bytes 772

commit v5 on v4

--- a/solution.py
+++ b/solution.py
@@ -16,11 +16,11 @@
 F32 = jnp.float32
 
 
-def halves(table):
+def halves(table, axis):
     table = np.asarray(table, np.float32)
     high = table.astype(ml_dtypes.bfloat16)
     low = (table - high.astype(np.float32)).astype(ml_dtypes.bfloat16)
-    return np.stack([high, low])
+    return np.concatenate([high, low, high], axis=axis)
 
 
 def turn(product, period):
@@ -117,23 +117,18 @@
     return out
 
 
-def split(x):
+def split(x, axis):
     high = x.astype(jnp.bfloat16)
-    return high, (x - high.astype(F32)).astype(jnp.bfloat16)
-
-
-def dot(a, b):
-    return jnp.dot(a, b, preferred_element_type=F32)
-
-
-def dot_right(x, table):
-    high, low = split(x)
-    return dot(high, table[0]) + (dot(low, table[0]) + dot(high, table[1]))
-
-
-def dot_left(table, x):
-    high, low = split(x)
-    return dot(table[0], high) + (dot(table[0], low) + dot(table[1], high))
+    low = (x - high.astype(F32)).astype(jnp.bfloat16)
+    return jnp.concatenate([high, high, low], axis=axis)
+
+
+def dot_right(x, table_ref):
+    return jnp.dot(split(x, 1), table_ref[...], preferred_element_type=F32)
+
+
+def dot_left(table_ref, x):
+    return jnp.dot(table_ref[...], split(x, 0), preferred_element_type=F32)
 
 
 def forward_kernel(x_ref, table_ref, first_ref, cos_ref, sin_ref, out_ref, held):
@@ -226,7 +221,7 @@
     slots = channels // WIDE // 2
     block = min(32, rows)
     table, first, cos, sin = channel_tables(channels)
-    tables = [jnp.asarray(halves(table)), jnp.asarray(halves(first)), jnp.asarray(cos), jnp.asarray(sin)]
+    tables = [jnp.asarray(halves(table, 0)), jnp.asarray(halves(first, 0)), jnp.asarray(cos), jnp.asarray(sin)]
     return pl.pallas_call(
         forward_kernel,
         grid=(rows // block,),
@@ -246,7 +241,7 @@
     width = channels // owners
     block = min(32, rows)
     table, first, cos, sin = channel_tables(channels)
-    tables = [jnp.asarray(halves(table.T)), jnp.asarray(halves(first.T)), jnp.asarray(cos), jnp.asarray(sin)]
+    tables = [jnp.asarray(halves(table.T, 0)), jnp.asarray(halves(first.T, 0)), jnp.asarray(cos), jnp.asarray(sin)]
     return pl.pallas_call(
         inverse_kernel,
         grid=(rows // block,),
@@ -260,12 +255,15 @@
     )(x, *tables)
 
 
+def distance(i, devices):
+    spread = math.gcd(4, devices)
+    return lax.rem(i, spread) * (devices // spread) + i // spread
+
+
 def others(devices, visit):
-    spread = math.gcd(4, devices)
-
     @pl.loop(1, devices)
     def _(i):
-        visit(lax.rem(i, spread) * (devices // spread) + i // spread)
+        visit(distance(i, devices))
 
 
 def greet(devices, owners, me):
@@ -423,11 +421,20 @@
         keep_part(q).start()
         others(devices, lambda step: everywhere(q, step).start())
 
-    def transform(side):
+    def some_halves(turn_at, turns):
+        share = -(-devices // turns)
+        for r in range(share):
+            i = turn_at * share + r
+
+            @pl.when((i > 0) & (i < devices))
+            def _():
+                half(distance(i, devices)).start()
+
+    def transform(side, between=None):
         time_kernel(
             lanes.at[side], turn_ref, cos_t_ref, sin_t_ref,
             factor_ref.at[:, :, pl.ds(side * LANES, LANES)], fir_ref, lanes.at[side],
-            line_held, padded,
+            line_held, padded, between,
         )
 
     take_own(0).start()
@@ -436,10 +443,9 @@
     take_own(0).wait()
     transform(0)
     keep_half().start()
-    others(devices, lambda step: half(step).start())
     take_own(1).wait()
-    transform(1)
-    ahead = min(2, chunks)
+    transform(1, some_halves)
+    ahead = min(4, chunks)
     for q in range(ahead):
         begin(q)
     keep_half().wait()
@@ -510,7 +516,7 @@
     block = min(CHUNK, rows)
     chunks = rows // block
     table, first, cos, sin = channel_tables(channels)
-    operands = [x] + [jnp.asarray(t) for t in (halves(table), halves(first), cos, sin)]
+    operands = [x] + [jnp.asarray(t) for t in (halves(table, 0), halves(first, 0), cos, sin)]
     buffers = [(owners, rows, width), (slots, block, 2 * WIDE), (chunks, slots, 2, block, WIDE)]
     scratch = [pltpu.VMEM(b, F32) for b in buffers] + exchange_semaphores(chunks, owners, devices)
     return exchange_call(send_out_kernel, 0, operands, (devices * chunks, 2, block, WIDE), scratch)
@@ -524,7 +530,7 @@
     rows = chunks * block
     table, first, cos, sin = channel_tables(channels)
     operands = [x, *time_tables(samples), factor, fir_table(taps)]
-    operands += [jnp.asarray(t) for t in (halves(table.T), halves(first.T), cos, sin)]
+    operands += [jnp.asarray(t) for t in (halves(table.T, 0), halves(first.T, 0), cos, sin)]
     shape = (owners, rows, channels // owners)
     buffers = [
         (2, pieces, 2, block, LANES), (2, samples // WIDE, WIDE, LANES),
@@ -538,7 +544,7 @@
     return exchange_call(send_back_kernel, 1, operands, shape, scratch)
 
 
-def time_kernel(x_ref, table_ref, cos_ref, sin_ref, factor_ref, fir_ref, out_ref, held, line):
+def time_kernel(x_ref, table_ref, cos_ref, sin_ref, factor_ref, fir_ref, out_ref, held, line, between=None):
     devices, _, rows, lanes = x_ref.shape
     radix = held.shape[1]
     per = WIDE // rows
@@ -558,6 +564,8 @@
 
     @pl.loop(0, radix)
     def _(g):
+        if between is not None:
+            between(g, 2 * radix)
         y = dot_left(table_ref, jnp.concatenate([held[0, g], held[1, g]], axis=1))
         factor = factor_ref[g]
         re = (y[:WIDE, :lanes] + y[WIDE:, lanes:]) * factor
@@ -585,6 +593,8 @@
 
     @pl.loop(0, radix)
     def _(b):
+        if between is not None:
+            between(radix + b, 2 * radix)
         at = pl.ds(pl.multiple_of(b * WIDE, WIDE), 2 * WIDE)
         y = dot_left(fir_ref, jnp.concatenate([line[0, at], line[1, at]], axis=1))
         to = pl.ds(b * per, per)
@@ -599,14 +609,14 @@
     row = jnp.pad(taps, (shift, period - count - shift))
     table = jnp.tile(row, WIDE)[: WIDE * 2 * WIDE].reshape(WIDE, 2 * WIDE)
     high = lax.reduce_precision(table, 8, 7)
-    return jnp.stack([high, table - high]).astype(jnp.bfloat16)
+    return jnp.concatenate([high, table - high, high], axis=1).astype(jnp.bfloat16)
 
 
 def time_tables(samples):
     radix = samples // WIDE
     a = np.arange(WIDE)
     cos, sin = turn(a[:, None] * a[None, :], WIDE)
-    table = jnp.asarray(halves(np.concatenate([cos, sin], axis=0)))
+    table = jnp.asarray(halves(np.concatenate([cos, sin], axis=0), 1))
     spread = (radix, WIDE, LANES)
     turns = turn(np.arange(radix)[:, None] * a[None, :], samples)
     return [table] + [

time: 502 us -> 509 us (1.014)
  Pallas kernels: 482 us -> 489 us
    pallas_call x2, Pallas kernels: 482 us -> 489 us  [exchange_call(): pl.pallas_call(kernel, in_specs=[anywhere] + [inside] * (len(operands) -...]
where the time goes in v5:
time: 509 us
  Pallas kernels  489 us (96%)
  other arithmetic  13.1 us (3%)
  local copies, waits for them, and re-layouts  6.39 us (1%)
    pallas_call x2, Pallas kernels, exchange_call(): pl.pallas_call(kernel, in_specs=[anywhere] + [inside] * (len(operands) -...  489 us

profile of v5, /device:TPU:1, one launch (start us, length us, event | category | flops | bytes accessed | tf_op | source)
XLA Modules:
  0.0 508.6 jit_solution(5922676561150610339)
XLA Ops:
  0.0 0.0 copy-start.3
  0.0 0.8 compare_select_fusion
  0.8 0.8 dynamic_slice.3
  1.5 0.9 reshape.27
  2.5 0.1 copy.21
  2.5 0.1 copy.22
  2.6 3.0 select_multiply_fusion.factor_ref
  5.6 0.0 copy-done.3
  5.6 0.1 pad.4
  5.7 0.5 tile.10
  6.3 0.1 reshape.28
  6.3 0.1 fusion
  6.4 0.9 pad_maximum_fusion.fir_ref
  7.4 0.0 copy-start.1
  7.4 0.0 copy-start
  7.4 205.5 %send_out_kernel.1.x_ref = f32[256,2,16,256]{3,2,1,0:T(8,128)} custom-call(f32[4,128,4096]{2,1,0:T(8,128)} %bitcast.8, bf16[1536,512]{1,0:T(8,128)(2,1)} %constant.49.clone.table_ref, bf16[1536,512]{1,0:T(8,128)(2,1)} %constant.50.clone.first_ref, f32[32,256]{1,0:T(8,128)} %constant.51.clone.cos_ref, f32[32,256]{1,0:T(8,128)} %constant.52.clone.sin_ref), custom_call_target="tpu_custom_call" | custom-call | tf_op jit(solution)/shard_map/send_out_kernel/pallas_call | solution.py:499
  212.9 0.0 copy-done.1
  212.9 1.9 jit_solution_.6.cos_t_ref
  214.8 0.0 copy-done
  214.8 1.9 jit_solution_.7.sin_t_ref
  216.7 0.0 copy-start.2
  216.7 0.0 copy-start.4
  216.7 283.5 %send_back_kernel.1 = f32[4,128,4096]{2,1,0:T(8,128)} custom-call(f32[256,2,16,256]{3,2,1,0:T(8,128)} %send_out_kernel.1.x_ref, bf16[512,768]{1,0:T(8,128)(2,1)} %constant.53.clone.turn_ref, f32[16,256,128]{2,1,0:T(8,128)} %jit_solution_.6.cos_t_ref, f32[16,256,128]{2,1,0:T(8,128)} %jit_solution_.7.sin_t_ref, ...), custom_call_target="tpu_custom_call" | custom-call | tf_op jit(solution)/shard_map/send_back_kernel/pallas_call | solution.py:499
  500.3 0.0 copy-done.2
  500.3 0.0 copy-done.4
  500.3 0.2 select_reduce_fusion
  500.5 8.1 %bitcast_multiply_fusion = f32[512,4096]{1,0:T(8,128)} fusion(f32[4,128,4096]{2,1,0:T(8,128)} %send_back_kernel.1, f32[4096]{0:T(1024)S(1)} %select_reduce_fusion), kind=kLoop, calls=%fused_computation | loop fusion | flops 2097152 | bytes 16793600 | tf_op jit(solution)/shard_map/mul | solution.py:705
  (3 shorter events, 0.1 us)
Async XLA Ops:
  0.0 5.6 %copy-start.3 = (f32[255]{0:T(256)S(1)}, f32[255]{0:T(256)}, u32[]{:S(2)}) copy-start(f32[255]{0:T(256)} %param.19) | copy-start | bytes 3064
  7.4 205.5 %copy-start.1 = (f32[16,256]{1,0:T(8,128)S(1)}, f32[16,256]{1,0:T(8,128)}, u32[]{:S(2)}) copy-start(f32[16,256]{1,0:T(8,128)} %constant.54.clone) | copy-start | bytes 49156
  7.4 207.4 %copy-start = (f32[16,256]{1,0:T(8,128)S(1)}, f32[16,256]{1,0:T(8,128)}, u32[]{:S(2)}) copy-start(f32[16,256]{1,0:T(8,128)} %constant.55.clone) | copy-start | bytes 49156
  216.7 283.5 %copy-start.2 = (s32[4096]{0:T(1024)S(1)}, s32[4096]{0:T(1024)}, u32[]{:S(2)}) copy-start(s32[4096]{0:T(1024)} %param.21) | copy-start | bytes 49156
  216.7 283.6 %copy-start.4 = (f32[64]{0:T(128)S(1)}, f32[64]{0:T(128)}, u32[]{:S(2)}) copy-start(f32[64]{0:T(128)} %param.20) | copy-start | bytes 772

commit v6 on v4

--- a/solution.py
+++ b/solution.py
@@ -556,18 +556,30 @@
             held[0, g, to] = re * c + im * s
             held[1, g, to] = im * c - re * s
 
-    @pl.loop(0, radix)
-    def _(g):
-        y = dot_left(table_ref, jnp.concatenate([held[0, g], held[1, g]], axis=1))
-        factor = factor_ref[g]
-        re = (y[:WIDE, :lanes] + y[WIDE:, lanes:]) * factor
-        im = (y[:WIDE, lanes:] - y[WIDE:, :lanes]) * factor
-        y = dot_left(table_ref, jnp.concatenate([re, im], axis=1))
-        re = y[:WIDE, :lanes] - y[WIDE:, lanes:]
-        im = y[:WIDE, lanes:] + y[WIDE:, :lanes]
-        c, s = cos_ref[g], sin_ref[g]
-        held[0, g] = re * c - im * s
-        held[1, g] = im * c + re * s
+    group = min(4, radix)
+
+    def columns(y, k):
+        return y[:, k * lanes : (k + 1) * lanes]
+
+    @pl.loop(0, radix // group)
+    def _(step):
+        gs = [step * group + k for k in range(group)]
+        x = jnp.concatenate([held[p, g] for g in gs for p in range(2)], axis=1)
+        y = dot_left(table_ref, x)
+        parts = []
+        for k, g in enumerate(gs):
+            factor = factor_ref[g]
+            cr, ci = columns(y[:WIDE], 2 * k), columns(y[:WIDE], 2 * k + 1)
+            sr, si = columns(y[WIDE:], 2 * k), columns(y[WIDE:], 2 * k + 1)
+            parts += [(cr + si) * factor, (ci - sr) * factor]
+        y = dot_left(table_ref, jnp.concatenate(parts, axis=1))
+        for k, g in enumerate(gs):
+            cr, ci = columns(y[:WIDE], 2 * k), columns(y[:WIDE], 2 * k + 1)
+            sr, si = columns(y[WIDE:], 2 * k), columns(y[WIDE:], 2 * k + 1)
+            re, im = cr - si, ci + sr
+            c, s = cos_ref[g], sin_ref[g]
+            held[0, g] = re * c - im * s
+            held[1, g] = im * c + re * s
 
     edge = line.shape[1] - LANES
     for part in range(2):
@@ -583,13 +595,17 @@
             line[0, to] = y[b][0]
             line[1, to] = y[b][1]
 
-    @pl.loop(0, radix)
-    def _(b):
-        at = pl.ds(pl.multiple_of(b * WIDE, WIDE), 2 * WIDE)
-        y = dot_left(fir_ref, jnp.concatenate([line[0, at], line[1, at]], axis=1))
-        to = pl.ds(b * per, per)
-        out_ref[to, 0] = y[:, :lanes].reshape(per, rows, lanes)
-        out_ref[to, 1] = y[:, lanes:].reshape(per, rows, lanes)
+    @pl.loop(0, radix // group)
+    def _(step):
+        bs = [step * group + k for k in range(group)]
+        x = [
+            line[p, pl.ds(pl.multiple_of(b * WIDE, WIDE), 2 * WIDE)] for b in bs for p in range(2)
+        ]
+        y = dot_left(fir_ref, jnp.concatenate(x, axis=1))
+        for k, b in enumerate(bs):
+            to = pl.ds(b * per, per)
+            out_ref[to, 0] = columns(y, 2 * k).reshape(per, rows, lanes)
+            out_ref[to, 1] = columns(y, 2 * k + 1).reshape(per, rows, lanes)
 
 
 def fir_table(taps):

time: 502 us -> 490 us (0.976)
  Pallas kernels: 482 us -> 471 us
    pallas_call x2, Pallas kernels: 482 us -> 471 us  [exchange_call(): pl.pallas_call(kernel, in_specs=[anywhere] + [inside] * (len(operands) -...]
where the time goes in v6:
time: 490 us
  Pallas kernels  471 us (96%)
  other arithmetic  13 us (3%)
  local copies, waits for them, and re-layouts  6.39 us (1%)
    pallas_call x2, Pallas kernels, exchange_call(): pl.pallas_call(kernel, in_specs=[anywhere] + [inside] * (len(operands) -...  471 us

profile of v6, /device:TPU:1, one launch (start us, length us, event | category | flops | bytes accessed | tf_op | source)
XLA Modules:
  0.0 490.1 jit_solution(2540349115307880062)
XLA Ops:
  0.0 0.0 copy-start.3
  0.0 0.8 compare_select_fusion
  0.8 0.8 dynamic_slice.3
  1.5 0.9 reshape.50
  2.5 0.1 copy.21
  2.5 0.1 copy.22
  2.6 3.0 select_multiply_fusion.factor_ref
  5.6 0.0 copy-done.3
  5.6 0.1 pad.4
  5.7 0.5 tile.10
  6.3 0.1 reshape.51
  6.3 0.1 reduce-precision_convert_fusion
  6.4 0.9 pad_maximum_fusion.fir_ref
  7.3 0.0 copy-start.1
  7.3 0.0 copy-start
  7.3 205.2 %send_out_kernel.1.x_ref = f32[256,2,16,256]{3,2,1,0:T(8,128)} custom-call(f32[4,128,4096]{2,1,0:T(8,128)} %bitcast.8, bf16[2,512,512]{2,1,0:T(8,128)(2,1)} %constant.49.clone.table_ref, bf16[2,512,512]{2,1,0:T(8,128)(2,1)} %constant.50.clone.first_ref, f32[32,256]{1,0:T(8,128)} %constant.51.clone.cos_ref, f32[32,256]{1,0:T(8,128)} %constant.52.clone.sin_ref), custom_call_target="tpu_custom_call" | custom-call | tf_op jit(solution)/shard_map/send_out_kernel/pallas_call | solution.py:493
  212.4 0.0 copy-done.1
  212.5 1.9 jit_solution_.6.cos_t_ref
  214.4 0.0 copy-done
  214.4 1.9 jit_solution_.7.sin_t_ref
  216.3 0.0 copy-start.2
  216.3 0.0 copy-start.4
  216.3 265.4 %send_back_kernel.1 = f32[4,128,4096]{2,1,0:T(8,128)} custom-call(f32[256,2,16,256]{3,2,1,0:T(8,128)} %send_out_kernel.1.x_ref, bf16[2,512,256]{2,1,0:T(8,128)(2,1)} %constant.53.clone.turn_ref, f32[16,256,128]{2,1,0:T(8,128)} %jit_solution_.6.cos_t_ref, f32[16,256,128]{2,1,0:T(8,128)} %jit_solution_.7.sin_t_ref, ...), custom_call_target="tpu_custom_call" | custom-call | tf_op jit(solution)/shard_map/send_back_kernel/pallas_call | solution.py:493
  481.7 0.0 copy-done.2
  481.7 0.0 copy-done.4
  481.7 0.2 select_reduce_fusion
  482.0 8.1 %bitcast_multiply_fusion = f32[512,4096]{1,0:T(8,128)} fusion(f32[4,128,4096]{2,1,0:T(8,128)} %send_back_kernel.1, f32[4096]{0:T(1024)S(1)} %select_reduce_fusion), kind=kLoop, calls=%fused_computation | loop fusion | flops 2097152 | bytes 16793600 | tf_op jit(solution)/shard_map/mul | solution.py:711
  (3 shorter events, 0.1 us)
Async XLA Ops:
  0.0 5.6 %copy-start.3 = (f32[255]{0:T(256)S(1)}, f32[255]{0:T(256)}, u32[]{:S(2)}) copy-start(f32[255]{0:T(256)} %param.19) | copy-start | bytes 3064
  7.3 205.2 %copy-start.1 = (f32[16,256]{1,0:T(8,128)S(1)}, f32[16,256]{1,0:T(8,128)}, u32[]{:S(2)}) copy-start(f32[16,256]{1,0:T(8,128)} %constant.54.clone) | copy-start | bytes 49156
  7.3 207.1 %copy-start = (f32[16,256]{1,0:T(8,128)S(1)}, f32[16,256]{1,0:T(8,128)}, u32[]{:S(2)}) copy-start(f32[16,256]{1,0:T(8,128)} %constant.55.clone) | copy-start | bytes 49156
  216.3 265.4 %copy-start.2 = (s32[4096]{0:T(1024)S(1)}, s32[4096]{0:T(1024)}, u32[]{:S(2)}) copy-start(s32[4096]{0:T(1024)} %param.21) | copy-start | bytes 49156
  216.3 265.4 %copy-start.4 = (f32[64]{0:T(128)S(1)}, f32[64]{0:T(128)}, u32[]{:S(2)}) copy-start(f32[64]{0:T(128)} %param.20) | copy-start | bytes 772
